TPU v7x, 128 devices: a whole 4x4x4 slice. The times are simulated.
128 devices in a mesh: gy: 32 (over x, y, core), gz: 4 (over z).
Axes of the slice: x: 4, y: 4, z: 4, core: 2. Of those that a mesh axis runs over, the one named last changes fastest.
Arguments:
- image: bfloat16 [128, 768, 128], P('gz', 'gy'), may hold values from -6 to 6
- labels: int32 [128, 768, 128], P('gz', 'gy'), may hold values from 0 to 2047
- brick_blocks: int32 [4, 32, 16], P('gz', 'gy'), may hold values from 0 to 127, as said below
- block_owner: int32 [128], replicated, may hold values from 0 to 31, as said below
Outputs:
- likeness: bfloat16 [128, 768, 128], P('gz', 'gy')
- label_features: float32 [128, 64, 128], P('gy', 'gz')
Inputs may be any that keep to these rules, and one draw needn't show every extreme that they name: `block_owner`: each index of gy owns exactly 4 blocks. `brick_blocks`: each brick lists 16 distinct blocks, no two of them with the same owner; one owner is listed by every brick.
All inputs are finite; a program needn't handle non-finite values.
Results may differ from a plain program's by a relative error of at most 0.009.
Values may be sent and summed in bfloat16 or wider, within the bound.
No kernel may reach another device: no remote copies, remote signals or barrier semaphores. Data moves between devices by JAX's collectives and lax.ppermute only.
A program may use at most 128 MiB of HBM per device.

v0:
```python
import math

import jax
import jax.numpy as jnp
from jax import lax
from jax.sharding import PartitionSpec as P

LBL = 128
FEAT = 64


CENTERS = (-1.5, -0.5, 0.5, 1.5)


def extended_2(shard, sides, width):
    for axis, dim in sides:
        size, length = (lax.axis_size(axis), shard.shape[dim])
        up = [(i, (i + 1) % size) for i in range(size - 1)]
        down = [(j, i) for i, j in up]
        last = lax.slice_in_dim(shard, length - width, length, axis=dim)
        leading = lax.slice_in_dim(shard, 0, width, axis=dim)
        before = lax.ppermute(last, axis, up)
        after = lax.ppermute(leading, axis, down)
        shard = jnp.concatenate([before, shard, after], axis=dim)
    return shard


def kernel_set(sigma_val):
    radius = 3 * sigma_val
    offsets = [float(step) for step in range(-radius, radius + 1)]
    smooth = [math.exp(-step * step / (2.0 * sigma_val**2)) for step in offsets]
    weight_total = sum(smooth)
    smooth = [value / weight_total for value in smooth]
    first_order = [step / sigma_val**2 * value for step, value in zip(offsets, smooth)]
    second = [
        (step * step / sigma_val**4 - 1.0 / sigma_val**2) * value
        for step, value in zip(offsets, smooth)
    ]
    return (radius, [smooth, first_order, second])


def along(volume_in, weights, dim_index, length_out):
    summed = weights[0] * lax.slice_in_dim(volume_in, 0, length_out, axis=dim_index)
    for tap_index in range(1, len(weights)):
        summed = summed + weights[tap_index] * lax.slice_in_dim(
            volume_in, tap_index, tap_index + length_out, axis=dim_index
        )
    return summed


def plane_pass(extended, sigma_val):
    radius, filters = kernel_set(sigma_val)
    inner_width = extended.shape[2]
    inner_rows = extended.shape[1] - 2 * radius
    padded = jnp.pad(extended, ((0, 0), (0, 0), (radius, radius)))
    along_x = [
        along(padded, filters[sorted_along_width], 2, inner_width)
        for sorted_along_width in range(3)
    ]
    combos = ((2, 0), (0, 2), (0, 0), (1, 1), (1, 0), (0, 1))
    return jnp.stack(
        [
            along(along_x[sorted_along_width], filters[order_y], 1, inner_rows)
            for sorted_along_width, order_y in combos
        ]
    )


def depth_pass(stacked, sigma_val):
    radius, filters = kernel_set(sigma_val)
    inner_depth = stacked.shape[1] - 2 * radius
    orders = (0, 0, 2, 0, 1, 1)
    return jnp.stack(
        [
            along(stacked[channel], filters[sorted_along_depth], 0, inner_depth)
            for channel, sorted_along_depth in enumerate(orders)
        ]
    )


def throat_channels(hessian, sigma_val):
    scaled = hessian * (4.0 * sigma_val**3.5)
    trace_sum = scaled[0] + scaled[1] + scaled[2]
    frobenius = (
        scaled[0] ** 2
        + scaled[1] ** 2
        + scaled[2] ** 2
        + 2.0 * (scaled[3] ** 2 + scaled[4] ** 2 + scaled[5] ** 2)
    )
    minors = 0.5 * (trace_sum * trace_sum - frobenius)
    tube_value = jnp.maximum(-trace_sum, 0.0) * jnp.maximum(minors, 0.0) / (frobenius + 0.25)
    return (jnp.concatenate([scaled, minors[None], tube_value[None]]), tube_value)


def feature_rows(feature_channels, volume):
    intensity_bands = jnp.stack([jnp.exp(-((volume - center) ** 2)) for center in CENTERS])
    mixed = feature_channels[:, None] * intensity_bands[None]
    return mixed.reshape(feature_channels.shape[0] * len(CENTERS), -1).astype(jnp.bfloat16)


def local(image, labels, brick_blocks, block_owner):
    slab_z, rows_y, width_x = image.shape
    groups = lax.axis_size("gy")
    depth_bundles = lax.axis_size("gz")
    listed_count = brick_blocks.shape[-1]
    volume = image.astype(jnp.float32)
    channel_list = []
    tube_list = []
    extended = extended_2(image, (("gy", 1), ("gz", 0)), 12).astype(jnp.float32)
    for sigma_val in (2, 4):
        radius = 3 * sigma_val
        inner = extended[12 - radius : 12 + slab_z + radius, 12 - radius : 12 + rows_y + radius]
        hessian = depth_pass(plane_pass(inner, sigma_val), sigma_val)
        feature_channels, tube_value = throat_channels(hessian, sigma_val)
        channel_list.append(feature_channels)
        tube_list.append(tube_value)
    likeness = jnp.maximum(tube_list[0], tube_list[1]).astype(jnp.bfloat16)
    feats = feature_rows(jnp.concatenate(channel_list), volume)
    local_flat = labels.reshape(-1)
    voxels = local_flat.shape[0]
    block_len = math.gcd(voxels, 4096)
    label_ids = jnp.arange(listed_count * LBL, dtype=jnp.int32)[:, None]

    def accumulate(turn_index, running):
        start = turn_index * block_len
        feat_block = lax.dynamic_slice_in_dim(feats, start, block_len, 1)
        marks = lax.dynamic_slice_in_dim(local_flat, start, block_len, 0)
        onehot = (marks[None, :] == label_ids).astype(jnp.bfloat16)
        return running + lax.dot_general(
            feat_block, onehot, (((1,), (1,)), ((), ())), preferred_element_type=jnp.float32
        )

    block_sums = lax.fori_loop(
        0, voxels // block_len, accumulate, jnp.zeros((FEAT, listed_count * LBL), jnp.float32)
    )
    partial_sums = block_sums.reshape(FEAT, listed_count, LBL).transpose(1, 0, 2)
    total_blocks = block_owner.shape[0]
    blk_dev = total_blocks // groups
    block_index = jnp.arange(total_blocks, dtype=jnp.int32)
    earlier = (block_index[None, :] < block_index[:, None]) & (
        block_owner[None, :] == block_owner[:, None]
    )
    owner_rank = jnp.sum(earlier.astype(jnp.int32), axis=1)
    slot_pos = block_owner * blk_dev + owner_rank
    listed_ids = brick_blocks.reshape(listed_count)
    listed = (listed_ids[:, None] == block_index[None, :]).astype(jnp.int32)
    my_pos = jnp.sum(listed * slot_pos[None, :], axis=1)
    placement_lookup = (block_index[:, None] == my_pos[None, :]).astype(jnp.float32)
    dense_table = jnp.einsum(
        "ia,aub->iub", placement_lookup, partial_sums, precision=lax.Precision.HIGHEST
    )
    quarter = FEAT // depth_bundles
    dense_table = dense_table.reshape(groups, blk_dev, depth_bundles, quarter, LBL).transpose(
        0, 2, 1, 3, 4
    )
    dense_table = dense_table.reshape(groups * depth_bundles * blk_dev, quarter, LBL)
    label_features = lax.psum_scatter(dense_table, ("gy", "gz"), scatter_dimension=0, tiled=True)
    return (likeness, label_features)


def solution(mesh):
    placed = (P("gz", "gy", None), P("gz", "gy", None), P("gz", "gy", None), P())
    return jax.shard_map(
        local,
        mesh=mesh,
        in_specs=placed,
        out_specs=(P("gz", "gy", None), P("gy", "gz", None)),
        check_vma=False,
    )
```

profile of v0, /device:TPU:1, one launch (start us, length us, event | category | flops | bytes accessed | tf_op | source)
XLA Modules:
  0.0 1013.4 jit_solution(17561973413435044582)
XLA Ops:
  7.2 1.0 fusion.319
  8.3 4.6 collective-permute-start
  12.9 1.9 collective-permute-start.1
  14.8 1.2 fusion.48
  16.4 2.8 collective-permute-done.1
  19.3 3.5 collective-permute-start.2
  22.8 1.3 collective-permute-start.3
  24.1 1.3 pad_maximum_fusion
  25.4 3.5 collective-permute-done.3
  28.9 1.2 fusion.316
  30.1 69.9 %multiply_add_fusion = (f32[56,48,128]{2,1,0:T(8,128)S(1)}, f32[56,48,128]{2,1,0:T(8,128)S(1)}, f32[56,48,128]{2,1,0:T(8,128)}) fusion(f32[56,48,128]{2,1,0:T(8,128)} %fusion.316, bf16[12,48,128]{2,1,0:T(8,128)(2,1)S(1)} %collective-permute-done.3, bf16[32,12,128]{2,1,0:T(8,128)(2,1)S(1)} %collective-permute-done.1, bf16[32,24,128]{2,1,0:T(8,128)(2,1)S(1)} %copy-done.3, ...), kind=kLoop, calls=%fused_computation.45 | loop fusion | flops 54018048 | bytes 6193152 | tf_op jit(solution)/shard_map/add | solution.py:45
  100.1 2.1 multiply_add_fusion.10
  102.2 2.1 multiply_add_fusion.9
  104.3 2.1 multiply_add_fusion.8
  106.4 2.1 multiply_add_fusion.7
  108.5 2.6 multiply_add_fusion.6
  111.1 8.8 multiply_add_fusion.3
  119.9 0.8 multiply_add_fusion.15
  120.8 0.8 multiply_add_fusion.14
  121.6 0.8 multiply_add_fusion.13
  122.4 0.8 multiply_add_fusion.12
  123.3 0.8 multiply_add_fusion.11
  124.6 2.2 fusion.7
  127.5 0.8 fusion.31
  134.8 1.2 copy-done.2
  136.0 6.8 multiply_convert_fusion
  142.8 13.6 %convert_element_type.32 = bf16[64,98304]{1,0:T(8,128)(2,1)} reshape(bf16[16,4,32,24,128]{4,3,2,1,0:T(8,128)(2,1)} %multiply_convert_fusion) | data formatting | bytes 25165824 | tf_op jit(solution)/shard_map/convert_element_type | solution.py:98
  156.4 206.0 %while.14 = (s32[]{:T(128)}, f32[64,2048]{1,0:T(8,128)S(1)}, bf16[64,98304]{1,0:T(8,128)(2,1)}, s32[98304]{0:T(1024)}, s32[]{:T(128)}, /*index=5*/s32[]{:T(128)}, s32[]{:T(128)}, s32[]{:T(128)}) while((s32[]{:T(128)}, f32[64,2048]{1,0:T(8,128)S(1)}, bf16[64,98304]{1,0:T(8,128)(2,1)}, s32[98304]{0:T(1024)}, s32[]{:T(128)}, ...), condition=%wide.region_3.4_spmd.clone, body=%wide.region_2.3_spmd.clone.sunk | while | flops 1082392576 | bytes 1622165 | solution.py:133
  156.6 0.7 dynamic_slice.21
  157.3 7.8 fusion.323
  165.2 0.7 dynamic_slice.21
  165.9 7.8 fusion.323
  173.8 0.7 dynamic_slice.21
  174.5 7.8 fusion.323
  182.3 0.7 dynamic_slice.21
  183.1 7.8 fusion.323
  190.9 0.7 dynamic_slice.21
  191.6 7.8 fusion.323
  200.2 7.8 fusion.323
  208.8 7.8 fusion.323
  216.7 0.7 dynamic_slice.21
  217.4 7.8 fusion.323
  226.0 7.8 fusion.323
  234.5 7.8 fusion.323
  243.1 7.8 fusion.323
  251.7 7.8 fusion.323
  260.3 7.8 fusion.323
  268.8 7.8 fusion.323
  276.7 0.7 dynamic_slice.21
  277.4 7.8 fusion.323
  285.3 0.7 dynamic_slice.21
  286.0 7.8 fusion.323
  294.6 7.8 fusion.323
  303.1 7.8 fusion.323
  311.7 7.8 fusion.323
  320.3 7.8 fusion.323
  328.9 7.8 fusion.323
  337.5 7.8 fusion.323
  345.3 0.7 dynamic_slice.21
  346.0 7.8 fusion.323
  354.6 7.8 fusion.323
  362.6 1.9 fusion.43
  364.5 4.4 copy.8
  369.6 636.7 %reduce-scatter.2.cloned.1.call-done = f32[4,16,128]{2,1,0:T(8,128)} async-done(((f32[512,16,128]{2,1,0:T(8,128)}), f32[4,16,128]{2,1,0:T(8,128)}) %reduce-scatter.2.cloned.1.call-update) | async-done | bytes 32784 | tf_op jit(solution)/shard_map/reduce_scatter | solution.py:157
  (58 shorter events, 19.8 us)
Async XLA Ops:
  7.2 12.0 %copy-start.3 = (bf16[32,24,128]{2,1,0:T(8,128)(2,1)S(1)}, bf16[32,24,128]{2,1,0:T(8,128)(2,1)}, u32[]{:S(2)}) copy-start(bf16[32,24,128]{2,1,0:T(8,128)(2,1)} %param.6) | copy-start | bytes 589828
  7.2 8.8 copy-start.5
  7.2 9.0 copy-start.6
  7.2 999.1 %reduce-scatter.2.cloned.1.call-start = ((), (), s32[]{:S(2)}) async-start(), calls=%async_computation.1 | async-start | bytes 4227072 | tf_op jit(solution)/shard_map/reduce_scatter | solution.py:157
  8.3 8.1 collective-permute-start
  12.9 6.3 collective-permute-start.1
  19.3 6.1 collective-permute-start.2
  22.8 6.1 collective-permute-start.3
  108.5 2.6 copy-start.1
  123.3 1.3 copy-start
  134.6 1.4 copy-start.2
  142.8 13.6 %copy-start.4 = (f32[64,2048]{1,0:T(8,128)S(1)}, f32[64,2048]{1,0:T(8,128)}, u32[]{:S(2)}) copy-start(f32[64,2048]{1,0:T(8,128)} %custom-call) | copy-start | bytes 1572868
Sparse Core Ops, SparseCore 0:
  369.0 637.2 reduce-scatter.1
where the time goes:
time: 1030 us; the launch traced here: 1010 us
  waiting for transfers between devices  643 us (62%)
  matrix products  190 us (18%)
  other arithmetic  115 us (11%)
  local copies, waits for them, and re-layouts  38.3 us (4%)
  between operations  14.6 us (1%)
  starting transfers between devices  11.4 us (1%)
    reduce_scatter x1, waiting for transfers between devices, local(): lax.psum_scatter(dense_table, ('gy', 'gz'), scatter_dimension=0, tiled=True)  637 us
    dot_general x24, matrix products, accumulate(): lax.dot_general(feat_block, onehot, (((1,), (1,)), ((), ())), preferred_e...  188 us
    add x14, other arithmetic, along(): summed + weights[tap_index] * lax.slice_in_dim(volume_in, tap_index, tap_...  96.9 us
  transfers between devices with their start and end apart: 5, of which 3 were waited for; matrix products, arithmetic and copies ran while one was open for 0% of the time, Pallas kernels for 0%

commit v1 on v0

v1 whole, which is shorter than its diff:
```python
import math

import jax
import jax.numpy as jnp
import ml_dtypes
import numpy as np
from jax import lax
from jax.experimental import pallas as pl
from jax.experimental.pallas import tpu as pltpu
from jax.sharding import PartitionSpec as P

LBL = 128
FEAT = 64
HALO = 12
ZC = 8
SIGMAS = (2, 4)
CENTERS = (-1.5, -0.5, 0.5, 1.5)
ORDERS = ((2, 0, 0), (0, 2, 0), (0, 0, 2), (1, 1, 0), (1, 0, 1), (0, 1, 1))
HI = 8
LO = 256
SEND = 24
F32, BF16 = jnp.float32, jnp.bfloat16


def kernel_set(sigma_val):
    radius = 3 * sigma_val
    offsets = [float(step) for step in range(-radius, radius + 1)]
    smooth = [math.exp(-step * step / (2.0 * sigma_val**2)) for step in offsets]
    weight_total = sum(smooth)
    smooth = [value / weight_total for value in smooth]
    first_order = [step / sigma_val**2 * value for step, value in zip(offsets, smooth)]
    second = [
        (step * step / sigma_val**4 - 1.0 / sigma_val**2) * value
        for step, value in zip(offsets, smooth)
    ]
    return (radius, [smooth, first_order, second])


def banded(weights, radius, rows, columns, offset):
    matrix = np.zeros((rows, columns))
    for row in range(rows):
        for tap, weight in enumerate(weights):
            column = row + offset + tap - radius
            if 0 <= column < columns:
                matrix[row, column] = weight
    return matrix


def two_parts(matrix):
    high = matrix.astype(np.float32).astype(ml_dtypes.bfloat16)
    low = (matrix - high.astype(np.float64)).astype(np.float32).astype(ml_dtypes.bfloat16)
    return (high, low)


def filter_matrices(rows_y, width):
    along_z, along_y, along_x = ([], [], [])
    for sigma_val in SIGMAS:
        radius, filters = kernel_set(sigma_val)
        y_rows = []
        for order in range(3):
            z_matrix = banded(filters[order], radius, ZC, ZC + 2 * HALO, HALO)
            along_z.append(np.kron(z_matrix, np.eye(8)))
            y_rows.append(banded(filters[order], radius, rows_y, rows_y + 2 * HALO, HALO))
            x_matrix = banded(filters[order], radius, width, width, 0).T
            high, low = two_parts(x_matrix * (4.0 * sigma_val**3.5))
            along_x.append(np.concatenate([high, high, low], axis=0))
        y_matrix = np.concatenate(y_rows)
        y_matrix = np.pad(y_matrix, ((0, -y_matrix.shape[0] % 16), (0, 0)))
        high, low = two_parts(y_matrix)
        along_y.append(np.concatenate([high, high, low], axis=1))
    z_high, z_low = two_parts(np.concatenate(along_z))
    return (np.stack([z_high, z_low]), np.stack(along_y), np.stack(along_x))


def split(value):
    high = value.astype(BF16)
    return (high, (value - high.astype(F32)).astype(BF16))


def throat_kernel(
    owner_ref, rank_ref, ext_ref, labels_ref, wz_ref, wy_ref, wx_ref,
    like_ref, send_ref,
    z_high, z_low, y_out, channels, bands, acc, turned,
):
    chunk = pl.program_id(0)
    rows_y = labels_ref.shape[1]
    deep = rows_y + 2 * HALO
    rows = ZC * rows_y
    width = labels_ref.shape[2]
    z_start = chunk * ZC

    for pair in range(deep // 16):
        tiles = [
            ext_ref[pl.ds(z_start, ZC + 2 * HALO), pl.ds(16 * pair + 8 * half, 8), :]
            .reshape((ZC + 2 * HALO) * 8, width)
            .astype(BF16)
            for half in range(2)
        ]
        grey = jnp.concatenate(tiles, axis=1)
        out = jnp.dot(wz_ref[0], grey, preferred_element_type=F32) + jnp.dot(
            wz_ref[1], grey, preferred_element_type=F32
        )
        out = out.reshape(6 * ZC, 8, 2 * width)
        out = jnp.concatenate([out[:, :, :width], out[:, :, width:]], axis=1)
        high, low = split(out)
        z_high[:, pl.ds(16 * pair, 16), :] = high
        z_low[:, pl.ds(16 * pair, 16), :] = low

    for scale in range(2):
        for order_z in range(3):
            for pair in range(ZC // 2):
                columns = []
                for half in range(2):
                    index = (scale * 3 + order_z) * ZC + 2 * pair + half
                    columns.append(
                        jnp.concatenate([z_high[index], z_low[index], z_high[index]], axis=0)
                    )
                deep_rows = jnp.concatenate(columns, axis=1)
                count = wy_ref.shape[1] if order_z == 0 else (48 if order_z == 1 else 32)
                out = jnp.dot(
                    wy_ref[scale, :count, :], deep_rows, preferred_element_type=F32
                )
                for order_y in range(3 - order_z):
                    component = [
                        i for i, o in enumerate(ORDERS) if o[1:] == (order_y, order_z)
                    ][0]
                    for half in range(2):
                        y_out[
                            scale * 6 + component, pl.ds((2 * pair + half) * rows_y, rows_y), :
                        ] = out[
                            order_y * rows_y : (order_y + 1) * rows_y,
                            half * width : (half + 1) * width,
                        ]

    tubes = []
    for scale in range(2):
        hessian = []
        for component, order in enumerate(ORDERS):
            high, low = split(y_out[scale * 6 + component])
            hessian.append(
                jnp.dot(
                    jnp.concatenate([high, low, high], axis=1),
                    wx_ref[scale * 3 + order[0]],
                    preferred_element_type=F32,
                )
            )
        xx, yy, zz, xy, xz, yz = hessian
        trace = xx + yy + zz
        frob = xx * xx + yy * yy + zz * zz + 2.0 * (xy * xy + xz * xz + yz * yz)
        minors = 0.5 * (trace * trace - frob)
        tube = jnp.maximum(-trace, 0.0) * jnp.maximum(minors, 0.0) / (frob + 0.25)
        tubes.append(tube)
        for index, value in enumerate(hessian + [minors, tube]):
            channels[pl.ds((scale * 8 + index) * rows, rows), :] = value
    like = jnp.maximum(tubes[0], tubes[1])
    like_ref[...] = like.reshape(ZC, rows_y, width).astype(BF16)

    volume = ext_ref[pl.ds(z_start + HALO, ZC), pl.ds(HALO, rows_y), :].astype(F32)
    volume = volume.reshape(rows, width)
    for index, center in enumerate(CENTERS):
        bands[pl.ds(index * rows, rows), :] = jnp.exp(-((volume - center) ** 2))

    @pl.when(chunk == 0)
    def _():
        acc[...] = jnp.zeros_like(acc)

    group = 8
    low_ids = lax.broadcasted_iota(jnp.int32, (LO, width), 0).astype(F32).astype(BF16)

    def step(index, carry):
        row0 = index * group
        plane = row0 // rows_y
        first = row0 - plane * rows_y
        left, right = ([], [])
        marks = labels_ref[plane, pl.ds(pl.multiple_of(first, 8), 8), :]
        mark_high = (marks >> 8).astype(F32)
        mark_low = (marks & 255).astype(F32)
        for row in range(group):
            feats = []
            for scale in range(2):
                base = channels[pl.ds(scale * 8 * rows + row0 + row, 8, stride=rows), :]
                for band in range(4):
                    gain = bands[pl.ds(band * rows + row0 + row, 1), :]
                    feats.append(base * gain)
            feats = jnp.concatenate(feats, axis=0).astype(BF16)
            high_of = jnp.broadcast_to(mark_high[row : row + 1], (FEAT, width)).astype(BF16)
            low_of = jnp.broadcast_to(mark_low[row : row + 1], (LO, width)).astype(BF16)
            zero = jnp.zeros_like(feats)
            left.append(
                jnp.concatenate(
                    [jnp.where(high_of == jnp.asarray(h, BF16), feats, zero) for h in range(HI)],
                    axis=0,
                )
            )
            right.append(
                jnp.where(low_of == low_ids, jnp.asarray(1, BF16), jnp.asarray(0, BF16))
            )
        acc[...] += lax.dot_general(
            jnp.concatenate(left, axis=1),
            jnp.concatenate(right, axis=1),
            (((1,), (1,)), ((), ())),
            preferred_element_type=F32,
        )
        return carry

    lax.fori_loop(0, rows // group, step, 0)

    @pl.when(chunk == pl.num_programs(0) - 1)
    def _():
        send_ref[...] = jnp.zeros_like(send_ref)
        for slot in range(owner_ref.shape[0]):
            owner = owner_ref[slot]
            rank = rank_ref[slot].astype(F32)
            for scale in range(2):
                for band in range(4):
                    turned[pl.ds(32 * scale + band, 8, stride=4), :] = acc[
                        pl.ds((slot // 2) * FEAT + 32 * scale + 8 * band, 8),
                        pl.ds((slot % 2) * LBL, LBL),
                    ]
            for quarter in range(4):
                send_ref[owner, quarter, pl.ds(0, 16), :] = turned[
                    pl.ds(16 * quarter, 16), :
                ].astype(BF16)
                send_ref[owner, quarter, pl.ds(16, 8), :] = jnp.full((8, LBL), rank, F32).astype(
                    BF16
                )


def sum_kernel(got_ref, out_ref):
    sources = got_ref.shape[0]

    def step(source, totals):
        block = got_ref[source].astype(F32)
        data, rank = (block[:16], jnp.concatenate([block[16:], block[16:]], axis=0))
        return tuple(
            total + jnp.where(rank == float(index), data, 0.0) for index, total in enumerate(totals)
        )

    totals = lax.fori_loop(
        0, sources, step, tuple(jnp.zeros(out_ref.shape[1:], F32) for _ in range(out_ref.shape[0]))
    )
    for index, total in enumerate(totals):
        out_ref[index] = total


def extended_2(shard, sides, width):
    for axis, dim in sides:
        size, length = (lax.axis_size(axis), shard.shape[dim])
        up = [(i, (i + 1) % size) for i in range(size - 1)]
        down = [(j, i) for i, j in up]
        last = lax.slice_in_dim(shard, length - width, length, axis=dim)
        leading = lax.slice_in_dim(shard, 0, width, axis=dim)
        before = lax.ppermute(last, axis, up)
        after = lax.ppermute(leading, axis, down)
        shard = jnp.concatenate([before, shard, after], axis=dim)
    return shard


def throat_sums(ext, labels, owners, ranks, groups, quarters):
    slab_z, rows_y, width = labels.shape
    matrices = filter_matrices(rows_y, width)
    rows = ZC * rows_y
    deep = rows_y + 2 * HALO
    whole = lambda array: pl.BlockSpec(array.shape, lambda i, *_: (0,) * array.ndim)
    return pl.pallas_call(
        throat_kernel,
        out_shape=(
            jax.ShapeDtypeStruct(labels.shape, BF16),
            jax.ShapeDtypeStruct((groups, quarters, SEND, LBL), BF16),
        ),
        grid_spec=pltpu.PrefetchScalarGridSpec(
            num_scalar_prefetch=2,
            grid=(slab_z // ZC,),
            in_specs=[
                whole(ext),
                pl.BlockSpec((ZC, rows_y, width), lambda i, *_: (i, 0, 0)),
                *[whole(matrix) for matrix in matrices],
            ],
            out_specs=(
                pl.BlockSpec((ZC, rows_y, width), lambda i, *_: (i, 0, 0)),
                pl.BlockSpec((groups, quarters, SEND, LBL), lambda i, *_: (0, 0, 0, 0)),
            ),
            scratch_shapes=[
                pltpu.VMEM((6 * ZC, deep, width), BF16),
                pltpu.VMEM((6 * ZC, deep, width), BF16),
                pltpu.VMEM((12, rows, width), F32),
                pltpu.VMEM((16 * rows, width), F32),
                pltpu.VMEM((4 * rows, width), F32),
                pltpu.VMEM((HI * FEAT, LO), F32),
                pltpu.VMEM((FEAT, LBL), F32),
            ],
        ),
        compiler_params=pltpu.CompilerParams(vmem_limit_bytes=48 * 1024 * 1024),
    )(owners, ranks, ext, labels, *matrices)


def local(image, labels, brick_blocks, block_owner):
    groups = lax.axis_size("gy")
    quarters = lax.axis_size("gz")
    listed_count = brick_blocks.shape[-1]
    total_blocks = block_owner.shape[0]
    blk_dev = total_blocks // groups
    block_index = jnp.arange(total_blocks, dtype=jnp.int32)
    earlier = (block_index[None, :] < block_index[:, None]) & (
        block_owner[None, :] == block_owner[:, None]
    )
    owner_rank = jnp.sum(earlier.astype(jnp.int32), axis=1)
    listed_ids = brick_blocks.reshape(listed_count)
    listed = (listed_ids[:, None] == block_index[None, :]).astype(jnp.int32)
    owners = jnp.sum(listed * block_owner[None, :], axis=1)
    ranks = jnp.sum(listed * owner_rank[None, :], axis=1)

    ext = extended_2(image, (("gy", 1), ("gz", 0)), HALO).astype(F32)
    likeness, message = throat_sums(ext, labels, owners, ranks, groups, quarters)
    message = message.reshape(groups * quarters, SEND, LBL)
    got = lax.all_to_all(message, ("gy", "gz"), 0, 0, tiled=True)
    label_features = pl.pallas_call(
        sum_kernel,
        out_shape=jax.ShapeDtypeStruct((blk_dev, FEAT // quarters, LBL), F32),
    )(got)
    return (likeness, label_features)


def solution(mesh):
    placed = (P("gz", "gy", None), P("gz", "gy", None), P("gz", "gy", None), P())
    return jax.shard_map(
        local,
        mesh=mesh,
        in_specs=placed,
        out_specs=(P("gz", "gy", None), P("gy", "gz", None)),
        check_vma=False,
    )
```

time: 1030 us -> 109 us (0.11); the launches traced: 1010 us -> 109 us
  waiting for transfers between devices: 643 us -> 7.35 us
  matrix products: 190 us -> 0 us
  other arithmetic: 115 us -> 2.92 us
  Pallas kernels: 0 us -> 58 us
  local copies, waits for them, and re-layouts: 38.3 us -> 1.12 us
  blocking collectives: 0 us -> 27.5 us
  between operations: 14.6 us -> 0.76 us
    reduce_scatter x1 -> x0, waiting for transfers between devices: 637 us -> none  [local(): lax.psum_scatter(dense_table, ('gy', 'gz'), scatter_dimension=0, tiled=True)]
    dot_general x25 -> x0, matrix products: 190 us -> none  [the longest x24 188 us: accumulate(): lax.dot_general(feat_block, onehot, (((1,), (1,)), ((), ())), preferred_e...]
    add x15 -> x0, other arithmetic: 96.9 us -> none  [the longest x14 96.9 us: along(): summed + weights[tap_index] * lax.slice_in_dim(volume_in, tap_index, tap_...]
    pallas_call x0 -> x2, Pallas kernels: none -> 58 us  [the longest x1 55.4 us: throat_sums(): pl.pallas_call(throat_kernel, out_shape=(jax.ShapeDtypeStruct(labels.shap...]
    all_to_all x0 -> x1, blocking collectives: none -> 27.5 us  [local(): got = lax.all_to_all(message, ('gy', 'gz'), 0, 0, tiled=True)]
    dynamic_slice x24 -> x0, local copies, waits for them, and re-layouts: 17.4 us -> none  [accumulate(): marks = lax.dynamic_slice_in_dim(local_flat, start, block_len, 0)]
    convert_element_type x1 -> x0, local copies, waits for them, and re-layouts: 13.6 us -> none  [feature_rows(): mixed.reshape(feature_channels.shape[0] * len(CENTERS), -1)]
  transfers between devices with their start and end apart: 5 -> 4, of which waited for: 3 -> 2; matrix products, arithmetic and copies ran while one was open for 0% -> 2% of each run, Pallas kernels for 0% -> 0%
where the time goes in v1:
time: 109 us
  Pallas kernels  58 us (53%)
  blocking collectives  27.5 us (25%)
  starting transfers between devices  11.5 us (11%)
  waiting for transfers between devices  7.35 us (7%)
  other arithmetic  2.92 us (3%)
  local copies, waits for them, and re-layouts  1.12 us (1%)
    pallas_call x1, Pallas kernels, throat_sums(): pl.pallas_call(throat_kernel, out_shape=(jax.ShapeDtypeStruct(labels.shap...  55.4 us
    all_to_all x1, blocking collectives, local(): got = lax.all_to_all(message, ('gy', 'gz'), 0, 0, tiled=True)  27.5 us
    ppermute x2, starting transfers between devices, extended_2(): before = lax.ppermute(last, axis, up)  8.14 us
    ppermute x2, waiting for transfers between devices, extended_2(): after = lax.ppermute(leading, axis, down)  7.34 us
    ppermute x2, starting transfers between devices, extended_2(): after = lax.ppermute(leading, axis, down)  3.34 us
    pallas_call x1, Pallas kernels, local(): pl.pallas_call(sum_kernel, out_shape=jax.ShapeDtypeStruct((blk_dev, FEAT...  2.62 us
  transfers between devices with their start and end apart: 4, of which 2 were waited for; matrix products, arithmetic and copies ran while one was open for 2% of the time, Pallas kernels for 0%

profile of v1, /device:TPU:1, one launch (start us, length us, event | category | flops | bytes accessed | tf_op | source)
XLA Modules:
  0.0 109.1 jit_solution(582252057533925360)
XLA Ops:
  0.6 0.0 copy-start.4
  0.6 1.1 fusion.1
  1.7 4.6 %collective-permute-start = (bf16[32,12,128]{2,1,0:T(8,128)(2,1)S(1)}, bf16[32,12,128]{2,1,0:T(8,128)(2,1)S(1)}, u32[]{:S(2)}, u32[]{:S(2)}) collective-permute-start(bf16[32,12,128]{2,1,0:T(8,128)(2,1)S(1)} %get-tuple-element.10), channel_id=1, source_target_pairs={{0,4},{4,8},{8,12},{12,16},{16,20},{20,24},{24,28},{28,32},{32,36}... | collective-permute-start | bytes 294920 | tf_op jit(solution)/shard_map/ppermute | solution.py:253
  6.3 0.0 copy-start
  6.3 0.0 copy-start.1
  6.4 0.0 copy-start.2
  6.4 0.0 copy-start.3
  6.4 2.1 %collective-permute-start.1 = (bf16[32,12,128]{2,1,0:T(8,128)(2,1)S(1)}, bf16[32,12,128]{2,1,0:T(8,128)(2,1)S(1)}, u32[]{:S(2)}, u32[]{:S(2)}) collective-permute-start(bf16[32,12,128]{2,1,0:T(8,128)(2,1)S(1)} %get-tuple-element.11), channel_id=1, source_target_pairs={{4,0},{8,4},{12,8},{16,12},{20,16},{24,20},{28,24},{32,28},{36,32}... | collective-permute-start | bytes 294920 | tf_op jit(solution)/shard_map/ppermute | solution.py:254
  8.4 0.0 collective-permute-done
  8.4 4.3 %collective-permute-done.1 = bf16[32,12,128]{2,1,0:T(8,128)(2,1)S(1)} collective-permute-done((bf16[32,12,128]{2,1,0:T(8,128)(2,1)S(1)}, bf16[32,12,128]{2,1,0:T(8,128)(2,1)S(1)}, u32[]{:S(2)}, u32[]{:S(2)}) %collective-permute-start.1) | collective-permute-done | bytes 98336 | tf_op jit(solution)/shard_map/ppermute | solution.py:254
  12.8 1.0 pad_maximum_fusion.2
  13.8 3.5 %collective-permute-start.2 = (bf16[12,48,128]{2,1,0:T(8,128)(2,1)S(1)}, bf16[12,48,128]{2,1,0:T(8,128)(2,1)S(1)}, u32[]{:S(2)}, u32[]{:S(2)}) collective-permute-start(bf16[12,48,128]{2,1,0:T(8,128)(2,1)S(1)} %get-tuple-element.8), channel_id=1, source_target_pairs={{0,1},{1,2},{2,3},{4,5},{5,6},{6,7},{8,9},{9,10},{10,11},{12,13},{... | collective-permute-start | bytes 442376 | tf_op jit(solution)/shard_map/ppermute | solution.py:253
  17.4 1.3 %collective-permute-start.3 = (bf16[12,48,128]{2,1,0:T(8,128)(2,1)S(1)}, bf16[12,48,128]{2,1,0:T(8,128)(2,1)S(1)}, u32[]{:S(2)}, u32[]{:S(2)}) collective-permute-start(bf16[12,48,128]{2,1,0:T(8,128)(2,1)S(1)} %get-tuple-element.9), channel_id=1, source_target_pairs={{1,0},{2,1},{3,2},{5,4},{6,5},{7,6},{9,8},{10,9},{11,10},{13,12},{... | collective-permute-start | bytes 442376 | tf_op jit(solution)/shard_map/ppermute | solution.py:254
  18.7 0.9 convert_reduce_fusion
  19.6 0.9 select_reduce_fusion
  20.4 0.0 collective-permute-done.2
  20.5 3.0 %collective-permute-done.3 = bf16[12,48,128]{2,1,0:T(8,128)(2,1)S(1)} collective-permute-done((bf16[12,48,128]{2,1,0:T(8,128)(2,1)S(1)}, bf16[12,48,128]{2,1,0:T(8,128)(2,1)S(1)}, u32[]{:S(2)}, u32[]{:S(2)}) %collective-permute-start.3) | collective-permute-done | bytes 147488 | tf_op jit(solution)/shard_map/ppermute | solution.py:254
  23.4 0.0 copy-done.4
  23.4 0.1 maximum_convert_fusion.ext_ref
  23.6 0.0 copy-done
  23.6 0.0 copy-done.1
  23.6 0.0 copy-done.2
  23.6 0.0 copy-done.3
  23.6 55.4 %shard_map.86 = (bf16[32,24,128]{2,1,0:T(8,128)(2,1)}, bf16[32,4,24,128]{3,2,1,0:T(8,128)(2,1)S(1)}) custom-call(s32[16]{0:T(128)S(1)} %get-tuple-element.7.owner_ref, s32[16]{0:T(128)S(1)} %get-tuple-element.6.rank_ref, f32[56,48,128]{2,1,0:T(8,128)S(1)} %maximum_convert_fusion.ext_ref, s32[32,24,128]{2,1,0:T(8,128)S(1)} %copy-done.1, ...), custom_call_target="tpu_custom_call" | custom-call | tf_op jit(solution)/shard_map/pallas_call | solution.py:265
  79.0 27.5 %all_to_all.5.got_ref = bf16[128,24,128]{2,1,0:T(8,128)(2,1)} all-to-all(bf16[128,24,128]{2,1,0:T(8,128)(2,1)S(1)} %bitcast.2), channel_id=1, replica_groups=mesh['gy'=32,'gz'=4] {'gy','gz'}, dimensions={0} | all-to-all | bytes 1572864 | tf_op jit(solution)/shard_map/all_to_all | solution.py:316
  106.5 2.6 %shard_map.87 = f32[4,16,128]{2,1,0:T(8,128)} custom-call(bf16[128,24,128]{2,1,0:T(8,128)(2,1)} %all_to_all.5.got_ref), custom_call_target="tpu_custom_call" | custom-call | tf_op jit(solution)/shard_map/pallas_call | solution.py:317
Async XLA Ops:
  0.6 22.8 %copy-start.4 = (bf16[32,24,128]{2,1,0:T(8,128)(2,1)S(1)}, bf16[32,24,128]{2,1,0:T(8,128)(2,1)}, u32[]{:S(2)}) copy-start(bf16[32,24,128]{2,1,0:T(8,128)(2,1)} %param.7) | copy-start | bytes 589828
  1.7 6.7 %collective-permute-start = (bf16[32,12,128]{2,1,0:T(8,128)(2,1)S(1)}, bf16[32,12,128]{2,1,0:T(8,128)(2,1)S(1)}, u32[]{:S(2)}, u32[]{:S(2)}) collective-permute-start(bf16[32,12,128]{2,1,0:T(8,128)(2,1)S(1)} %get-tuple-element.10), channel_id=1, source_target_pairs={{0,4},{4,8},{8,12},{12,16},{16,20},{20,24},{24,28},{28,32},{32,36}... | collective-permute-start | bytes 294920 | tf_op jit(solution)/shard_map/ppermute | solution.py:253
  6.3 17.3 %copy-start = (bf16[6,384,128]{2,1,0:T(8,128)(2,1)S(1)}, bf16[6,384,128]{2,1,0:T(8,128)(2,1)}, u32[]{:S(2)}) copy-start(bf16[6,384,128]{2,1,0:T(8,128)(2,1)} %constant.12.clone.wx_ref) | copy-start | bytes 1769476
  6.3 17.3 %copy-start.1 = (s32[32,24,128]{2,1,0:T(8,128)S(1)}, s32[32,24,128]{2,1,0:T(8,128)}, u32[]{:S(2)}) copy-start(s32[32,24,128]{2,1,0:T(8,128)} %labels_ref.1) | copy-start | bytes 1179652
  6.4 17.3 %copy-start.2 = (bf16[2,384,256]{2,1,0:T(8,128)(2,1)S(1)}, bf16[2,384,256]{2,1,0:T(8,128)(2,1)}, u32[]{:S(2)}) copy-start(bf16[2,384,256]{2,1,0:T(8,128)(2,1)} %constant.10.clone.wz_ref) | copy-start | bytes 1179652
  6.4 17.3 %copy-start.3 = (bf16[2,80,144]{2,1,0:T(8,128)(2,1)S(1)}, bf16[2,80,144]{2,1,0:T(8,128)(2,1)}, u32[]{:S(2)}) copy-start(bf16[2,80,144]{2,1,0:T(8,128)(2,1)} %constant.11.clone.wy_ref) | copy-start | bytes 138244
  6.4 6.4 %collective-permute-start.1 = (bf16[32,12,128]{2,1,0:T(8,128)(2,1)S(1)}, bf16[32,12,128]{2,1,0:T(8,128)(2,1)S(1)}, u32[]{:S(2)}, u32[]{:S(2)}) collective-permute-start(bf16[32,12,128]{2,1,0:T(8,128)(2,1)S(1)} %get-tuple-element.11), channel_id=1, source_target_pairs={{4,0},{8,4},{12,8},{16,12},{20,16},{24,20},{28,24},{32,28},{36,32}... | collective-permute-start | bytes 294920 | tf_op jit(solution)/shard_map/ppermute | solution.py:254
  13.8 6.6 %collective-permute-start.2 = (bf16[12,48,128]{2,1,0:T(8,128)(2,1)S(1)}, bf16[12,48,128]{2,1,0:T(8,128)(2,1)S(1)}, u32[]{:S(2)}, u32[]{:S(2)}) collective-permute-start(bf16[12,48,128]{2,1,0:T(8,128)(2,1)S(1)} %get-tuple-element.8), channel_id=1, source_target_pairs={{0,1},{1,2},{2,3},{4,5},{5,6},{6,7},{8,9},{9,10},{10,11},{12,13},{... | collective-permute-start | bytes 442376 | tf_op jit(solution)/shard_map/ppermute | solution.py:253
  17.4 6.1 %collective-permute-start.3 = (bf16[12,48,128]{2,1,0:T(8,128)(2,1)S(1)}, bf16[12,48,128]{2,1,0:T(8,128)(2,1)S(1)}, u32[]{:S(2)}, u32[]{:S(2)}) collective-permute-start(bf16[12,48,128]{2,1,0:T(8,128)(2,1)S(1)} %get-tuple-element.9), channel_id=1, source_target_pairs={{1,0},{2,1},{3,2},{5,4},{6,5},{7,6},{9,8},{10,9},{11,10},{13,12},{... | collective-permute-start | bytes 442376 | tf_op jit(solution)/shard_map/ppermute | solution.py:254

commit v2 on v1

--- a/solution.py
+++ b/solution.py
@@ -12,7 +12,8 @@
 LBL = 128
 FEAT = 64
 HALO = 12
-ZC = 8
+ZC = 4
+PLANES = 4
 SIGMAS = (2, 4)
 CENTERS = (-1.5, -0.5, 0.5, 1.5)
 ORDERS = ((2, 0, 0), (0, 2, 0), (0, 0, 2), (1, 1, 0), (1, 0, 1), (0, 1, 1))
@@ -77,21 +78,14 @@
     return (high, (value - high.astype(F32)).astype(BF16))
 
 
-def throat_kernel(
-    owner_ref, rank_ref, ext_ref, labels_ref, wz_ref, wy_ref, wx_ref,
-    like_ref, send_ref,
-    z_high, z_low, y_out, channels, bands, acc, turned,
-):
-    chunk = pl.program_id(0)
-    rows_y = labels_ref.shape[1]
+def filters_of(z_start, ext, wz_ref, wy_ref, wx_ref, z_high, z_low, y_out, channels, bands, like_ref):
+    rows_y, width = like_ref.shape[1:]
     deep = rows_y + 2 * HALO
     rows = ZC * rows_y
-    width = labels_ref.shape[2]
-    z_start = chunk * ZC
 
     for pair in range(deep // 16):
         tiles = [
-            ext_ref[pl.ds(z_start, ZC + 2 * HALO), pl.ds(16 * pair + 8 * half, 8), :]
+            ext[pl.ds(z_start, ZC + 2 * HALO), pl.ds(16 * pair + 8 * half, 8), :]
             .reshape((ZC + 2 * HALO) * 8, width)
             .astype(BF16)
             for half in range(2)
@@ -153,35 +147,30 @@
         for index, value in enumerate(hessian + [minors, tube]):
             channels[pl.ds((scale * 8 + index) * rows, rows), :] = value
     like = jnp.maximum(tubes[0], tubes[1])
-    like_ref[...] = like.reshape(ZC, rows_y, width).astype(BF16)
-
-    volume = ext_ref[pl.ds(z_start + HALO, ZC), pl.ds(HALO, rows_y), :].astype(F32)
-    volume = volume.reshape(rows, width)
+    like_ref[pl.ds(z_start, ZC)] = like.reshape(ZC, rows_y, width).astype(BF16)
+
+    volume = ext[pl.ds(z_start + HALO, ZC), pl.ds(HALO, rows_y), :].reshape(rows, width)
     for index, center in enumerate(CENTERS):
         bands[pl.ds(index * rows, rows), :] = jnp.exp(-((volume - center) ** 2))
 
-    @pl.when(chunk == 0)
-    def _():
-        acc[...] = jnp.zeros_like(acc)
-
-    group = 8
+
+def add_sums(z_start, labels_ref, channels, bands, acc):
+    rows_y, width = labels_ref.shape[1:]
+    rows = ZC * rows_y
+    group = PLANES * rows_y
     low_ids = lax.broadcasted_iota(jnp.int32, (LO, width), 0).astype(F32).astype(BF16)
-
-    def step(index, carry):
-        row0 = index * group
-        plane = row0 // rows_y
-        first = row0 - plane * rows_y
+    for part in range(ZC // PLANES):
         left, right = ([], [])
-        marks = labels_ref[plane, pl.ds(pl.multiple_of(first, 8), 8), :]
+        marks = labels_ref[pl.ds(z_start + part * PLANES, PLANES)].reshape(group, width)
         mark_high = (marks >> 8).astype(F32)
         mark_low = (marks & 255).astype(F32)
         for row in range(group):
+            at = part * group + row
             feats = []
             for scale in range(2):
-                base = channels[pl.ds(scale * 8 * rows + row0 + row, 8, stride=rows), :]
+                base = channels[pl.ds(scale * 8 * rows + at, 8, stride=rows), :]
                 for band in range(4):
-                    gain = bands[pl.ds(band * rows + row0 + row, 1), :]
-                    feats.append(base * gain)
+                    feats.append(base * bands[pl.ds(band * rows + at, 1), :])
             feats = jnp.concatenate(feats, axis=0).astype(BF16)
             high_of = jnp.broadcast_to(mark_high[row : row + 1], (FEAT, width)).astype(BF16)
             low_of = jnp.broadcast_to(mark_low[row : row + 1], (LO, width)).astype(BF16)
@@ -201,29 +190,80 @@
             (((1,), (1,)), ((), ())),
             preferred_element_type=F32,
         )
+
+
+def inner_kernel(
+    own_ref, labels_ref, wz_ref, wy_ref, wx_ref,
+    like_ref, acc,
+    ext, z_high, z_low, y_out, channels_0, channels_1, bands_0, bands_1,
+):
+    slab_z = labels_ref.shape[0]
+    ext[pl.ds(HALO, slab_z)] = own_ref[...].astype(F32)
+    acc[...] = jnp.zeros_like(acc)
+    buffers = ((channels_0, bands_0), (channels_1, bands_1))
+    starts = range(HALO, slab_z - HALO, ZC)
+    for index, z_start in enumerate(starts):
+        filters_of(
+            z_start, ext, wz_ref, wy_ref, wx_ref, z_high, z_low, y_out,
+            *buffers[index % 2], like_ref,
+        )
+        if index:
+            add_sums(z_start - ZC, labels_ref, *buffers[(index - 1) % 2], acc)
+    add_sums(starts[-1], labels_ref, *buffers[(len(starts) - 1) % 2], acc)
+
+
+def outer_kernel(
+    owner_ref, rank_ref, before_ref, own_ref, after_ref, labels_ref, wz_ref, wy_ref, wx_ref,
+    inner_like_ref, inner_acc_ref,
+    like_ref, send_ref,
+    ext, z_high, z_low, y_out, channels_0, channels_1, bands_0, bands_1, acc, turned,
+):
+    slab_z = labels_ref.shape[0]
+    ext[pl.ds(0, HALO)] = before_ref[...].astype(F32)
+    ext[pl.ds(HALO, slab_z)] = own_ref[...].astype(F32)
+    ext[pl.ds(HALO + slab_z, HALO)] = after_ref[...].astype(F32)
+    acc[...] = inner_acc_ref[...]
+    inner = pl.ds(HALO, slab_z - 2 * HALO)
+    like_ref[inner] = inner_like_ref[inner]
+    half = HALO // ZC
+    count = 2 * half
+
+    def start_of(index):
+        return index * ZC + jnp.where(index >= half, slab_z - 2 * HALO, 0)
+
+    def filters(index, channels, bands):
+        filters_of(
+            start_of(index), ext, wz_ref, wy_ref, wx_ref, z_high, z_low, y_out,
+            channels, bands, like_ref,
+        )
+
+    filters(jnp.int32(0), channels_0, bands_0)
+
+    def step(index, carry):
+        first = 2 * index
+        filters(first + 1, channels_1, bands_1)
+        add_sums(start_of(first), labels_ref, channels_0, bands_0, acc)
+        filters(jnp.minimum(first + 2, count - 1), channels_0, bands_0)
+        add_sums(start_of(first + 1), labels_ref, channels_1, bands_1, acc)
         return carry
 
-    lax.fori_loop(0, rows // group, step, 0)
-
-    @pl.when(chunk == pl.num_programs(0) - 1)
-    def _():
-        send_ref[...] = jnp.zeros_like(send_ref)
-        for slot in range(owner_ref.shape[0]):
-            owner = owner_ref[slot]
-            rank = rank_ref[slot].astype(F32)
-            for scale in range(2):
-                for band in range(4):
-                    turned[pl.ds(32 * scale + band, 8, stride=4), :] = acc[
-                        pl.ds((slot // 2) * FEAT + 32 * scale + 8 * band, 8),
-                        pl.ds((slot % 2) * LBL, LBL),
-                    ]
-            for quarter in range(4):
-                send_ref[owner, quarter, pl.ds(0, 16), :] = turned[
-                    pl.ds(16 * quarter, 16), :
-                ].astype(BF16)
-                send_ref[owner, quarter, pl.ds(16, 8), :] = jnp.full((8, LBL), rank, F32).astype(
-                    BF16
-                )
+    lax.fori_loop(0, count // 2, step, 0)
+
+    send_ref[...] = jnp.zeros_like(send_ref)
+    for slot in range(owner_ref.shape[0]):
+        owner = owner_ref[slot]
+        rank = rank_ref[slot].astype(F32)
+        for scale in range(2):
+            for band in range(4):
+                turned[pl.ds(32 * scale + band, 8, stride=4), :] = acc[
+                    pl.ds((slot // 2) * FEAT + 32 * scale + 8 * band, 8),
+                    pl.ds((slot % 2) * LBL, LBL),
+                ]
+        for quarter in range(4):
+            send_ref[owner, quarter, pl.ds(0, 16), :] = turned[pl.ds(16 * quarter, 16), :].astype(
+                BF16
+            )
+            send_ref[owner, quarter, pl.ds(16, 8), :] = jnp.full((8, LBL), rank, F32).astype(BF16)
 
 
 def sum_kernel(got_ref, out_ref):
@@ -237,61 +277,82 @@
         )
 
     totals = lax.fori_loop(
-        0, sources, step, tuple(jnp.zeros(out_ref.shape[1:], F32) for _ in range(out_ref.shape[0]))
+        0,
+        sources,
+        step,
+        tuple(jnp.zeros(out_ref.shape[1:], F32) for _ in range(out_ref.shape[0])),
+        unroll=8,
     )
     for index, total in enumerate(totals):
         out_ref[index] = total
 
 
-def extended_2(shard, sides, width):
-    for axis, dim in sides:
-        size, length = (lax.axis_size(axis), shard.shape[dim])
-        up = [(i, (i + 1) % size) for i in range(size - 1)]
-        down = [(j, i) for i, j in up]
-        last = lax.slice_in_dim(shard, length - width, length, axis=dim)
-        leading = lax.slice_in_dim(shard, 0, width, axis=dim)
-        before = lax.ppermute(last, axis, up)
-        after = lax.ppermute(leading, axis, down)
-        shard = jnp.concatenate([before, shard, after], axis=dim)
-    return shard
-
-
-def throat_sums(ext, labels, owners, ranks, groups, quarters):
-    slab_z, rows_y, width = labels.shape
-    matrices = filter_matrices(rows_y, width)
+def extended(shard, axis, dim, width):
+    size, length = (lax.axis_size(axis), shard.shape[dim])
+    up = [(i, (i + 1) % size) for i in range(size - 1)]
+    down = [(j, i) for i, j in up]
+    last = lax.slice_in_dim(shard, length - width, length, axis=dim)
+    leading = lax.slice_in_dim(shard, 0, width, axis=dim)
+    return (lax.ppermute(last, axis, up), lax.ppermute(leading, axis, down))
+
+
+VMEM = pl.BlockSpec(memory_space=pltpu.VMEM)
+SMEM = pl.BlockSpec(memory_space=pltpu.SMEM)
+
+
+def scratch(slab_z, rows_y, width):
     rows = ZC * rows_y
     deep = rows_y + 2 * HALO
-    whole = lambda array: pl.BlockSpec(array.shape, lambda i, *_: (0,) * array.ndim)
+    return [
+        pltpu.VMEM((slab_z + 2 * HALO, deep, width), F32),
+        pltpu.VMEM((6 * ZC, deep, width), BF16),
+        pltpu.VMEM((6 * ZC, deep, width), BF16),
+        pltpu.VMEM((12, rows, width), F32),
+        pltpu.VMEM((16 * rows, width), F32),
+        pltpu.VMEM((16 * rows, width), F32),
+        pltpu.VMEM((4 * rows, width), F32),
+        pltpu.VMEM((4 * rows, width), F32),
+    ]
+
+
+def cost(share):
+    return pl.CostEstimate(
+        flops=int(share * 28e9), bytes_accessed=int(share * 4e6), transcendentals=int(share * 4e5)
+    )
+
+
+PARAMS = pltpu.CompilerParams(vmem_limit_bytes=58 * 1024 * 1024)
+
+
+def inner_sums(own, labels, matrices):
     return pl.pallas_call(
-        throat_kernel,
+        inner_kernel,
+        out_shape=(
+            jax.ShapeDtypeStruct(labels.shape, BF16),
+            jax.ShapeDtypeStruct((HI * FEAT, LO), F32),
+        ),
+        in_specs=[VMEM] * 5,
+        out_specs=(VMEM, VMEM),
+        scratch_shapes=scratch(*labels.shape),
+        compiler_params=PARAMS,
+        cost_estimate=cost(0.25),
+    )(own, labels, *matrices)
+
+
+def outer_sums(owners, ranks, before, own, after, labels, matrices, inner, groups, quarters):
+    return pl.pallas_call(
+        outer_kernel,
         out_shape=(
             jax.ShapeDtypeStruct(labels.shape, BF16),
             jax.ShapeDtypeStruct((groups, quarters, SEND, LBL), BF16),
         ),
-        grid_spec=pltpu.PrefetchScalarGridSpec(
-            num_scalar_prefetch=2,
-            grid=(slab_z // ZC,),
-            in_specs=[
-                whole(ext),
-                pl.BlockSpec((ZC, rows_y, width), lambda i, *_: (i, 0, 0)),
-                *[whole(matrix) for matrix in matrices],
-            ],
-            out_specs=(
-                pl.BlockSpec((ZC, rows_y, width), lambda i, *_: (i, 0, 0)),
-                pl.BlockSpec((groups, quarters, SEND, LBL), lambda i, *_: (0, 0, 0, 0)),
-            ),
-            scratch_shapes=[
-                pltpu.VMEM((6 * ZC, deep, width), BF16),
-                pltpu.VMEM((6 * ZC, deep, width), BF16),
-                pltpu.VMEM((12, rows, width), F32),
-                pltpu.VMEM((16 * rows, width), F32),
-                pltpu.VMEM((4 * rows, width), F32),
-                pltpu.VMEM((HI * FEAT, LO), F32),
-                pltpu.VMEM((FEAT, LBL), F32),
-            ],
-        ),
-        compiler_params=pltpu.CompilerParams(vmem_limit_bytes=48 * 1024 * 1024),
-    )(owners, ranks, ext, labels, *matrices)
+        in_specs=[SMEM] * 2 + [VMEM] * 9,
+        out_specs=(VMEM, VMEM),
+        scratch_shapes=scratch(*labels.shape)
+        + [pltpu.VMEM((HI * FEAT, LO), F32), pltpu.VMEM((FEAT, LBL), F32)],
+        compiler_params=PARAMS,
+        cost_estimate=cost(0.75),
+    )(owners, ranks, before, own, after, labels, *matrices, *inner)
 
 
 def local(image, labels, brick_blocks, block_owner):
@@ -310,8 +371,14 @@
     owners = jnp.sum(listed * block_owner[None, :], axis=1)
     ranks = jnp.sum(listed * owner_rank[None, :], axis=1)
 
-    ext = extended_2(image, (("gy", 1), ("gz", 0)), HALO).astype(F32)
-    likeness, message = throat_sums(ext, labels, owners, ranks, groups, quarters)
+    matrices = filter_matrices(*labels.shape[1:])
+    left, right = extended(image, "gy", 1, HALO)
+    own = jnp.concatenate([left, image, right], axis=1)
+    before, after = extended(own, "gz", 0, HALO)
+    inner = inner_sums(own, labels, matrices)
+    likeness, message = outer_sums(
+        owners, ranks, before, own, after, labels, matrices, inner, groups, quarters
+    )
     message = message.reshape(groups * quarters, SEND, LBL)
     got = lax.all_to_all(message, ("gy", "gz"), 0, 0, tiled=True)
     label_features = pl.pallas_call(

time: 109 us -> 90.7 us (0.83)
  Pallas kernels: 58 us -> 43.5 us
  waiting for transfers between devices: 7.35 us -> 2.82 us
  other arithmetic: 2.92 us -> 1 us
  local copies, waits for them, and re-layouts: 1.12 us -> 2.48 us
    pallas_call x1 -> x2, Pallas kernels: 55.4 us -> 41.3 us  [the longest x1 29.6 us: outer_sums(): pl.pallas_call(outer_kernel, out_shape=(jax.ShapeDtypeStruct(labels.shape...]
    ppermute x4, waiting for transfers between devices: 7.35 us -> 2.82 us  [extended(): return (lax.ppermute(last, axis, up), lax.ppermute(leading, axis, down))]
    unnamed x10 -> x12, local copies, waits for them, and re-layouts: 0.03 us -> 1.38 us
  transfers between devices with their start and end apart: 4 -> 4, of which waited for: 2 -> 1; matrix products, arithmetic and copies ran while one was open for 2% -> 1% of each run, Pallas kernels for 0% -> 13%
where the time goes in v2:
time: 90.7 us; the launch traced here: 90.3 us
  Pallas kernels  43.5 us (48%)
  blocking collectives  27.9 us (31%)
  starting transfers between devices  12 us (13%)
  waiting for transfers between devices  2.82 us (3%)
  local copies, waits for them, and re-layouts  2.48 us (3%)
  other arithmetic  1 us (1%)
    pallas_call x1, Pallas kernels, outer_sums(): pl.pallas_call(outer_kernel, out_shape=(jax.ShapeDtypeStruct(labels.shape...  29.6 us
    all_to_all x1, blocking collectives, local(): got = lax.all_to_all(message, ('gy', 'gz'), 0, 0, tiled=True)  27.9 us
    ppermute x4, starting transfers between devices, extended(): return (lax.ppermute(last, axis, up), lax.ppermute(leading, axis, down))  12 us
    pallas_call x1, Pallas kernels, inner_sums(): pl.pallas_call(inner_kernel, out_shape=(jax.ShapeDtypeStruct(labels.shape...  11.6 us
    ppermute x4, waiting for transfers between devices, extended(): return (lax.ppermute(last, axis, up), lax.ppermute(leading, axis, down))  2.82 us
    pallas_call x1, Pallas kernels, local(): pl.pallas_call(sum_kernel, out_shape=jax.ShapeDtypeStruct((blk_dev, FEAT...  2.19 us
  transfers between devices with their start and end apart: 4, of which 1 were waited for; matrix products, arithmetic and copies ran while one was open for 1% of the time, Pallas kernels for 13%

profile of v2, /device:TPU:1, one launch (start us, length us, event | category | flops | bytes accessed | tf_op | source)
XLA Modules:
  0.0 90.3 jit_solution(18115801090396165146)
XLA Ops:
  0.6 0.0 copy-start.1
  0.6 1.1 %fusion.2 = (bf16[32,12,128]{2,1,0:T(8,128)(2,1)S(1)}, bf16[32,12,128]{2,1,0:T(8,128)(2,1)S(1)}) fusion(bf16[32,24,128]{2,1,0:T(8,128)(2,1)} %param.7), kind=kLoop, calls=%fused_computation.8 | loop fusion | bytes 393216 | tf_op jit(solution)/shard_map/slice | solution.py:294
  1.7 0.0 copy-start.2
  1.7 4.6 %collective-permute-start = (bf16[32,12,128]{2,1,0:T(8,128)(2,1)S(1)}, bf16[32,12,128]{2,1,0:T(8,128)(2,1)S(1)}, u32[]{:S(2)}, u32[]{:S(2)}) collective-permute-start(bf16[32,12,128]{2,1,0:T(8,128)(2,1)S(1)} %get-tuple-element.14), channel_id=1, source_target_pairs={{0,4},{4,8},{8,12},{12,16},{16,20},{20,24},{24,28},{28,32},{32,36}... | collective-permute-start | bytes 294920 | tf_op jit(solution)/shard_map/ppermute | solution.py:296
  6.3 1.9 %collective-permute-start.1 = (bf16[32,12,128]{2,1,0:T(8,128)(2,1)S(1)}, bf16[32,12,128]{2,1,0:T(8,128)(2,1)S(1)}, u32[]{:S(2)}, u32[]{:S(2)}) collective-permute-start(bf16[32,12,128]{2,1,0:T(8,128)(2,1)S(1)} %get-tuple-element.15), channel_id=1, source_target_pairs={{4,0},{8,4},{12,8},{16,12},{20,16},{24,20},{28,24},{32,28},{36,32}... | collective-permute-start | bytes 294920 | tf_op jit(solution)/shard_map/ppermute | solution.py:296
  8.3 0.0 copy-done.2
  8.3 0.2 convert_reduce_fusion
  8.5 0.0 copy-start.3
  8.5 0.7 copy-done.3
  9.1 0.7 select_reduce_fusion
  9.8 0.0 collective-permute-done
  9.8 2.8 %collective-permute-done.1 = bf16[32,12,128]{2,1,0:T(8,128)(2,1)S(1)} collective-permute-done((bf16[32,12,128]{2,1,0:T(8,128)(2,1)S(1)}, bf16[32,12,128]{2,1,0:T(8,128)(2,1)S(1)}, u32[]{:S(2)}, u32[]{:S(2)}) %collective-permute-start.1) | collective-permute-done | bytes 98336 | tf_op jit(solution)/shard_map/ppermute | solution.py:296
  12.6 0.0 copy-done.1
  12.6 0.1 pad_maximum_fusion.own_ref
  12.8 0.0 copy-start
  12.8 1.3 %collective-permute-start.3 = (bf16[12,48,128]{2,1,0:T(8,128)(2,1)S(1)}, bf16[12,48,128]{2,1,0:T(8,128)(2,1)S(1)}, u32[]{:S(2)}, u32[]{:S(2)}) collective-permute-start(bf16[12,48,128]{2,1,0:T(8,128)(2,1)S(1)} %get-tuple-element.12), channel_id=1, source_target_pairs={{1,0},{2,1},{3,2},{5,4},{6,5},{7,6},{9,8},{10,9},{11,10},{13,12},{... | collective-permute-start | bytes 442376 | tf_op jit(solution)/shard_map/ppermute | solution.py:296
  14.1 4.2 %collective-permute-start.2 = (bf16[12,48,128]{2,1,0:T(8,128)(2,1)S(1)}, bf16[12,48,128]{2,1,0:T(8,128)(2,1)S(1)}, u32[]{:S(2)}, u32[]{:S(2)}) collective-permute-start(bf16[12,48,128]{2,1,0:T(8,128)(2,1)S(1)} %get-tuple-element.13), channel_id=1, source_target_pairs={{0,1},{1,2},{2,3},{4,5},{5,6},{6,7},{8,9},{9,10},{10,11},{12,13},{... | collective-permute-start | bytes 442376 | tf_op jit(solution)/shard_map/ppermute | solution.py:296
  18.3 0.0 copy-done
  18.3 11.6 %shard_map.86 = (bf16[32,24,128]{2,1,0:T(8,128)(2,1)}, f32[512,256]{1,0:T(8,128)}) custom-call(bf16[32,48,128]{2,1,0:T(8,128)(2,1)} %copy-done, s32[32,24,128]{2,1,0:T(8,128)} %labels_ref.3, bf16[2,192,224]{2,1,0:T(8,128)(2,1)} %constant.10.clone.wz_ref, bf16[2,80,144]{2,1,0:T(8,128)(2,1)} %constant.11.clone.wy_ref, bf16[6,384,128]{2,1,0:T(8,128)(2,1)} %constant.12.clone.wx_ref), custom_call_target="tpu_custom_call" | custom-call | flops 7000000000 | bytes 1000000 | tf_op jit(solution)/shard_map/pallas_call | solution.py:328
  29.9 0.0 collective-permute-done.3.after_ref
  29.9 0.0 copy-start.4
  30.0 0.0 collective-permute-done.2.before_ref
  30.0 0.0 copy-start.5
  30.0 0.6 copy-done.4
  30.6 0.1 copy-done.5
  30.7 29.6 %shard_map.87 = (bf16[32,24,128]{2,1,0:T(8,128)(2,1)}, bf16[32,4,24,128]{3,2,1,0:T(8,128)(2,1)}) custom-call(s32[16]{0:T(128)} %get-tuple-element.11.owner_ref, s32[16]{0:T(128)} %get-tuple-element.10.rank_ref, bf16[12,48,128]{2,1,0:T(8,128)(2,1)} %copy-done.5, bf16[32,48,128]{2,1,0:T(8,128)(2,1)} %copy-done, bf16[12,48,128]{2,1,0:T(8,128)(2,1)} %copy-done.4, ...), custom_call_target="tpu_custom_call" | custom-call | flops 20999999488 | bytes 3000000 | tf_op jit(solution)/shard_map/pallas_call | solution.py:343
  60.3 27.9 %all_to_all.5.got_ref = bf16[128,24,128]{2,1,0:T(8,128)(2,1)} all-to-all(bf16[128,24,128]{2,1,0:T(8,128)(2,1)} %bitcast.2), channel_id=1, replica_groups=mesh['gy'=32,'gz'=4] {'gy','gz'}, dimensions={0} | all-to-all | bytes 1572864 | tf_op jit(solution)/shard_map/all_to_all | solution.py:383
  88.2 2.2 %shard_map.88 = f32[4,16,128]{2,1,0:T(8,128)} custom-call(bf16[128,24,128]{2,1,0:T(8,128)(2,1)} %all_to_all.5.got_ref), custom_call_target="tpu_custom_call" | custom-call | tf_op jit(solution)/shard_map/pallas_call | solution.py:384
  (1 shorter events, 0.0 us)
Async XLA Ops:
  0.6 12.0 %copy-start.1 = (bf16[32,24,128]{2,1,0:T(8,128)(2,1)S(1)}, bf16[32,24,128]{2,1,0:T(8,128)(2,1)}, u32[]{:S(2)}) copy-start(bf16[32,24,128]{2,1,0:T(8,128)(2,1)} %param.7) | copy-start | bytes 589828
  1.7 6.5 %copy-start.2 = (s32[128]{0:T(128)S(1)}, s32[128]{0:T(128)}, u32[]{:S(2)}) copy-start(s32[128]{0:T(128)} %param.10) | copy-start | bytes 1540
  1.7 8.1 %collective-permute-start = (bf16[32,12,128]{2,1,0:T(8,128)(2,1)S(1)}, bf16[32,12,128]{2,1,0:T(8,128)(2,1)S(1)}, u32[]{:S(2)}, u32[]{:S(2)}) collective-permute-start(bf16[32,12,128]{2,1,0:T(8,128)(2,1)S(1)} %get-tuple-element.14), channel_id=1, source_target_pairs={{0,4},{4,8},{8,12},{12,16},{16,20},{20,24},{24,28},{28,32},{32,36}... | collective-permute-start | bytes 294920 | tf_op jit(solution)/shard_map/ppermute | solution.py:296
  6.3 6.3 %collective-permute-start.1 = (bf16[32,12,128]{2,1,0:T(8,128)(2,1)S(1)}, bf16[32,12,128]{2,1,0:T(8,128)(2,1)S(1)}, u32[]{:S(2)}, u32[]{:S(2)}) collective-permute-start(bf16[32,12,128]{2,1,0:T(8,128)(2,1)S(1)} %get-tuple-element.15), channel_id=1, source_target_pairs={{4,0},{8,4},{12,8},{16,12},{20,16},{24,20},{28,24},{32,28},{36,32}... | collective-permute-start | bytes 294920 | tf_op jit(solution)/shard_map/ppermute | solution.py:296
  8.5 0.7 copy-start.3
  12.8 5.5 %copy-start = (bf16[32,48,128]{2,1,0:T(8,128)(2,1)}, bf16[32,48,128]{2,1,0:T(8,128)(2,1)S(1)}, u32[]{:S(2)}) copy-start(bf16[32,48,128]{2,1,0:T(8,128)(2,1)S(1)} %pad_maximum_fusion.own_ref) | copy-start | bytes 1179652
  12.8 17.1 %collective-permute-start.3 = (bf16[12,48,128]{2,1,0:T(8,128)(2,1)S(1)}, bf16[12,48,128]{2,1,0:T(8,128)(2,1)S(1)}, u32[]{:S(2)}, u32[]{:S(2)}) collective-permute-start(bf16[12,48,128]{2,1,0:T(8,128)(2,1)S(1)} %get-tuple-element.12), channel_id=1, source_target_pairs={{1,0},{2,1},{3,2},{5,4},{6,5},{7,6},{9,8},{10,9},{11,10},{13,12},{... | collective-permute-start | bytes 442376 | tf_op jit(solution)/shard_map/ppermute | solution.py:296
  14.1 15.8 %collective-permute-start.2 = (bf16[12,48,128]{2,1,0:T(8,128)(2,1)S(1)}, bf16[12,48,128]{2,1,0:T(8,128)(2,1)S(1)}, u32[]{:S(2)}, u32[]{:S(2)}) collective-permute-start(bf16[12,48,128]{2,1,0:T(8,128)(2,1)S(1)} %get-tuple-element.13), channel_id=1, source_target_pairs={{0,1},{1,2},{2,3},{4,5},{5,6},{6,7},{8,9},{9,10},{10,11},{12,13},{... | collective-permute-start | bytes 442376 | tf_op jit(solution)/shard_map/ppermute | solution.py:296
  29.9 0.7 copy-start.4
  30.0 0.7 copy-start.5

commit v3 on v2

--- a/solution.py
+++ b/solution.py
@@ -12,8 +12,8 @@
 LBL = 128
 FEAT = 64
 HALO = 12
-ZC = 4
-PLANES = 4
+ZC_IN, ZC_OUT = (8, 6)
+PLANES_IN, PLANES_OUT = (4, 3)
 SIGMAS = (2, 4)
 CENTERS = (-1.5, -0.5, 0.5, 1.5)
 ORDERS = ((2, 0, 0), (0, 2, 0), (0, 0, 2), (1, 1, 0), (1, 0, 1), (0, 1, 1))
@@ -53,24 +53,24 @@
     return (high, low)
 
 
-def filter_matrices(rows_y, width):
+def filter_matrices(chunk, rows_y, width):
     along_z, along_y, along_x = ([], [], [])
     for sigma_val in SIGMAS:
         radius, filters = kernel_set(sigma_val)
         y_rows = []
         for order in range(3):
-            z_matrix = banded(filters[order], radius, ZC, ZC + 2 * HALO, HALO)
+            z_matrix = banded(filters[order], radius, chunk, chunk + 2 * HALO, HALO)
             along_z.append(np.kron(z_matrix, np.eye(8)))
             y_rows.append(banded(filters[order], radius, rows_y, rows_y + 2 * HALO, HALO))
             x_matrix = banded(filters[order], radius, width, width, 0).T
-            high, low = two_parts(x_matrix * (4.0 * sigma_val**3.5))
-            along_x.append(np.concatenate([high, high, low], axis=0))
+            parts = np.concatenate(two_parts(x_matrix * (4.0 * sigma_val**3.5)), axis=1)
+            along_x.append(np.concatenate([parts, parts], axis=0))
         y_matrix = np.concatenate(y_rows)
         y_matrix = np.pad(y_matrix, ((0, -y_matrix.shape[0] % 16), (0, 0)))
         high, low = two_parts(y_matrix)
         along_y.append(np.concatenate([high, high, low], axis=1))
-    z_high, z_low = two_parts(np.concatenate(along_z))
-    return (np.stack([z_high, z_low]), np.stack(along_y), np.stack(along_x))
+    z_parts = np.concatenate(two_parts(np.concatenate(along_z)), axis=0)
+    return (z_parts, np.stack(along_y), np.stack(along_x))
 
 
 def split(value):
@@ -78,23 +78,23 @@
     return (high, (value - high.astype(F32)).astype(BF16))
 
 
-def filters_of(z_start, ext, wz_ref, wy_ref, wx_ref, z_high, z_low, y_out, channels, bands, like_ref):
+def filters_of(
+    z_start, chunk, ext, wz_ref, wy_ref, wx_ref, z_high, z_low, y_out, channels, bands, like_ref
+):
     rows_y, width = like_ref.shape[1:]
     deep = rows_y + 2 * HALO
-    rows = ZC * rows_y
+    rows = chunk * rows_y
+    planes = 6 * chunk
 
     for pair in range(deep // 16):
         tiles = [
-            ext[pl.ds(z_start, ZC + 2 * HALO), pl.ds(16 * pair + 8 * half, 8), :]
-            .reshape((ZC + 2 * HALO) * 8, width)
+            ext[pl.ds(z_start, chunk + 2 * HALO), pl.ds(16 * pair + 8 * half, 8), :]
+            .reshape((chunk + 2 * HALO) * 8, width)
             .astype(BF16)
             for half in range(2)
         ]
-        grey = jnp.concatenate(tiles, axis=1)
-        out = jnp.dot(wz_ref[0], grey, preferred_element_type=F32) + jnp.dot(
-            wz_ref[1], grey, preferred_element_type=F32
-        )
-        out = out.reshape(6 * ZC, 8, 2 * width)
+        out = jnp.dot(wz_ref[...], jnp.concatenate(tiles, axis=1), preferred_element_type=F32)
+        out = (out[: planes * 8] + out[planes * 8 :]).reshape(planes, 8, 2 * width)
         out = jnp.concatenate([out[:, :, :width], out[:, :, width:]], axis=1)
         high, low = split(out)
         z_high[:, pl.ds(16 * pair, 16), :] = high
@@ -102,10 +102,10 @@
 
     for scale in range(2):
         for order_z in range(3):
-            for pair in range(ZC // 2):
+            for pair in range(chunk // 2):
                 columns = []
                 for half in range(2):
-                    index = (scale * 3 + order_z) * ZC + 2 * pair + half
+                    index = (scale * 3 + order_z) * chunk + 2 * pair + half
                     columns.append(
                         jnp.concatenate([z_high[index], z_low[index], z_high[index]], axis=0)
                     )
@@ -128,16 +128,18 @@
 
     tubes = []
     for scale in range(2):
-        hessian = []
-        for component, order in enumerate(ORDERS):
-            high, low = split(y_out[scale * 6 + component])
-            hessian.append(
-                jnp.dot(
-                    jnp.concatenate([high, low, high], axis=1),
-                    wx_ref[scale * 3 + order[0]],
-                    preferred_element_type=F32,
-                )
+        hessian = [None] * 6
+        for order_x in range(3):
+            members = [i for i, o in enumerate(ORDERS) if o[0] == order_x]
+            two = [jnp.concatenate(split(y_out[scale * 6 + i]), axis=1) for i in members]
+            out = jnp.dot(
+                jnp.concatenate(two, axis=0),
+                wx_ref[scale * 3 + order_x],
+                preferred_element_type=F32,
             )
+            out = out[:, :width] + out[:, width:]
+            for index, member in enumerate(members):
+                hessian[member] = out[index * rows : (index + 1) * rows]
         xx, yy, zz, xy, xz, yz = hessian
         trace = xx + yy + zz
         frob = xx * xx + yy * yy + zz * zz + 2.0 * (xy * xy + xz * xz + yz * yz)
@@ -147,21 +149,22 @@
         for index, value in enumerate(hessian + [minors, tube]):
             channels[pl.ds((scale * 8 + index) * rows, rows), :] = value
     like = jnp.maximum(tubes[0], tubes[1])
-    like_ref[pl.ds(z_start, ZC)] = like.reshape(ZC, rows_y, width).astype(BF16)
-
-    volume = ext[pl.ds(z_start + HALO, ZC), pl.ds(HALO, rows_y), :].reshape(rows, width)
+    like_ref[pl.ds(z_start, chunk)] = like.reshape(chunk, rows_y, width).astype(BF16)
+
+    volume = ext[pl.ds(z_start + HALO, chunk), pl.ds(HALO, rows_y), :].reshape(rows, width)
     for index, center in enumerate(CENTERS):
         bands[pl.ds(index * rows, rows), :] = jnp.exp(-((volume - center) ** 2))
 
 
-def add_sums(z_start, labels_ref, channels, bands, acc):
+def add_sums(z_start, chunk, planes, labels_ref, channels, bands, acc):
     rows_y, width = labels_ref.shape[1:]
-    rows = ZC * rows_y
-    group = PLANES * rows_y
+    rows = chunk * rows_y
+    group = planes * rows_y
     low_ids = lax.broadcasted_iota(jnp.int32, (LO, width), 0).astype(F32).astype(BF16)
-    for part in range(ZC // PLANES):
+
+    def step(part, carry):
         left, right = ([], [])
-        marks = labels_ref[pl.ds(z_start + part * PLANES, PLANES)].reshape(group, width)
+        marks = labels_ref[pl.ds(z_start + part * planes, planes)].reshape(group, width)
         mark_high = (marks >> 8).astype(F32)
         mark_low = (marks & 255).astype(F32)
         for row in range(group):
@@ -190,64 +193,59 @@
             (((1,), (1,)), ((), ())),
             preferred_element_type=F32,
         )
+        return carry
+
+    lax.fori_loop(0, chunk // planes, step, 0)
+
+
+def all_chunks(start_of, count, chunk, planes, ext, labels_ref, weights, passes, buffers, acc, like_ref):
+    def step(index, carry):
+        z_start = start_of(index)
+        filters_of(z_start, chunk, ext, *weights, *passes, *buffers, like_ref)
+        add_sums(z_start, chunk, planes, labels_ref, *buffers, acc)
+        return carry
+
+    lax.fori_loop(0, count, step, 0)
 
 
 def inner_kernel(
     own_ref, labels_ref, wz_ref, wy_ref, wx_ref,
     like_ref, acc,
-    ext, z_high, z_low, y_out, channels_0, channels_1, bands_0, bands_1,
+    ext, z_high, z_low, y_out, channels, bands,
 ):
     slab_z = labels_ref.shape[0]
     ext[pl.ds(HALO, slab_z)] = own_ref[...].astype(F32)
     acc[...] = jnp.zeros_like(acc)
-    buffers = ((channels_0, bands_0), (channels_1, bands_1))
-    starts = range(HALO, slab_z - HALO, ZC)
-    for index, z_start in enumerate(starts):
-        filters_of(
-            z_start, ext, wz_ref, wy_ref, wx_ref, z_high, z_low, y_out,
-            *buffers[index % 2], like_ref,
-        )
-        if index:
-            add_sums(z_start - ZC, labels_ref, *buffers[(index - 1) % 2], acc)
-    add_sums(starts[-1], labels_ref, *buffers[(len(starts) - 1) % 2], acc)
+    all_chunks(
+        lambda index: HALO + index * ZC_IN, (slab_z - 2 * HALO) // ZC_IN, ZC_IN, PLANES_IN, ext, labels_ref,
+        (wz_ref, wy_ref, wx_ref), (z_high, z_low, y_out),
+        (channels, bands), acc, like_ref,
+    )
 
 
 def outer_kernel(
-    owner_ref, rank_ref, before_ref, own_ref, after_ref, labels_ref, wz_ref, wy_ref, wx_ref,
-    inner_like_ref, inner_acc_ref,
+    owner_ref, rank_ref, ends_ref, before_ref, own_ref, after_ref, labels_ref, wz_ref, wy_ref,
+    wx_ref, inner_like_ref, inner_acc_ref,
     like_ref, send_ref,
-    ext, z_high, z_low, y_out, channels_0, channels_1, bands_0, bands_1, acc, turned,
+    ext, z_high, z_low, y_out, channels, bands, acc, turned,
 ):
     slab_z = labels_ref.shape[0]
-    ext[pl.ds(0, HALO)] = before_ref[...].astype(F32)
     ext[pl.ds(HALO, slab_z)] = own_ref[...].astype(F32)
-    ext[pl.ds(HALO + slab_z, HALO)] = after_ref[...].astype(F32)
+    for end, (ref, at) in enumerate(((before_ref, 0), (after_ref, HALO + slab_z))):
+        ext[pl.ds(at, HALO)] = jnp.where(ends_ref[end] != 0, 0.0, ref[...].astype(F32))
     acc[...] = inner_acc_ref[...]
     inner = pl.ds(HALO, slab_z - 2 * HALO)
     like_ref[inner] = inner_like_ref[inner]
-    half = HALO // ZC
-    count = 2 * half
+    half = HALO // ZC_OUT
 
     def start_of(index):
-        return index * ZC + jnp.where(index >= half, slab_z - 2 * HALO, 0)
-
-    def filters(index, channels, bands):
-        filters_of(
-            start_of(index), ext, wz_ref, wy_ref, wx_ref, z_high, z_low, y_out,
-            channels, bands, like_ref,
-        )
-
-    filters(jnp.int32(0), channels_0, bands_0)
-
-    def step(index, carry):
-        first = 2 * index
-        filters(first + 1, channels_1, bands_1)
-        add_sums(start_of(first), labels_ref, channels_0, bands_0, acc)
-        filters(jnp.minimum(first + 2, count - 1), channels_0, bands_0)
-        add_sums(start_of(first + 1), labels_ref, channels_1, bands_1, acc)
-        return carry
-
-    lax.fori_loop(0, count // 2, step, 0)
+        return index * ZC_OUT + jnp.where(index >= half, slab_z - 2 * HALO, 0)
+
+    all_chunks(
+        start_of, 2 * half, ZC_OUT, PLANES_OUT, ext, labels_ref,
+        (wz_ref, wy_ref, wx_ref), (z_high, z_low, y_out),
+        (channels, bands), acc, like_ref,
+    )
 
     send_ref[...] = jnp.zeros_like(send_ref)
     for slot in range(owner_ref.shape[0]):
@@ -287,30 +285,30 @@
         out_ref[index] = total
 
 
-def extended(shard, axis, dim, width):
+def neighbours(shard, axis, dim, width):
     size, length = (lax.axis_size(axis), shard.shape[dim])
-    up = [(i, (i + 1) % size) for i in range(size - 1)]
+    up = [(i, (i + 1) % size) for i in range(size)]
     down = [(j, i) for i, j in up]
     last = lax.slice_in_dim(shard, length - width, length, axis=dim)
     leading = lax.slice_in_dim(shard, 0, width, axis=dim)
-    return (lax.ppermute(last, axis, up), lax.ppermute(leading, axis, down))
+    here = lax.axis_index(axis)
+    ends = (here == 0, here == size - 1)
+    return (lax.ppermute(last, axis, up), lax.ppermute(leading, axis, down), ends)
 
 
 VMEM = pl.BlockSpec(memory_space=pltpu.VMEM)
 SMEM = pl.BlockSpec(memory_space=pltpu.SMEM)
 
 
-def scratch(slab_z, rows_y, width):
-    rows = ZC * rows_y
+def scratch(chunk, slab_z, rows_y, width):
+    rows = chunk * rows_y
     deep = rows_y + 2 * HALO
     return [
         pltpu.VMEM((slab_z + 2 * HALO, deep, width), F32),
-        pltpu.VMEM((6 * ZC, deep, width), BF16),
-        pltpu.VMEM((6 * ZC, deep, width), BF16),
+        pltpu.VMEM((6 * chunk, deep, width), BF16),
+        pltpu.VMEM((6 * chunk, deep, width), BF16),
         pltpu.VMEM((12, rows, width), F32),
         pltpu.VMEM((16 * rows, width), F32),
-        pltpu.VMEM((16 * rows, width), F32),
-        pltpu.VMEM((4 * rows, width), F32),
         pltpu.VMEM((4 * rows, width), F32),
     ]
 
@@ -321,10 +319,11 @@
     )
 
 
-PARAMS = pltpu.CompilerParams(vmem_limit_bytes=58 * 1024 * 1024)
-
-
-def inner_sums(own, labels, matrices):
+PARAMS = pltpu.CompilerParams(vmem_limit_bytes=36 * 1024 * 1024)
+
+
+def inner_sums(own, labels):
+    matrices = filter_matrices(ZC_IN, *labels.shape[1:])
     return pl.pallas_call(
         inner_kernel,
         out_shape=(
@@ -333,26 +332,27 @@
         ),
         in_specs=[VMEM] * 5,
         out_specs=(VMEM, VMEM),
-        scratch_shapes=scratch(*labels.shape),
+        scratch_shapes=scratch(ZC_IN, *labels.shape),
         compiler_params=PARAMS,
         cost_estimate=cost(0.25),
     )(own, labels, *matrices)
 
 
-def outer_sums(owners, ranks, before, own, after, labels, matrices, inner, groups, quarters):
+def outer_sums(owners, ranks, ends, before, own, after, labels, inner, groups, quarters):
+    matrices = filter_matrices(ZC_OUT, *labels.shape[1:])
     return pl.pallas_call(
         outer_kernel,
         out_shape=(
             jax.ShapeDtypeStruct(labels.shape, BF16),
             jax.ShapeDtypeStruct((groups, quarters, SEND, LBL), BF16),
         ),
-        in_specs=[SMEM] * 2 + [VMEM] * 9,
+        in_specs=[SMEM] * 3 + [VMEM] * 9,
         out_specs=(VMEM, VMEM),
-        scratch_shapes=scratch(*labels.shape)
+        scratch_shapes=scratch(ZC_OUT, *labels.shape)
         + [pltpu.VMEM((HI * FEAT, LO), F32), pltpu.VMEM((FEAT, LBL), F32)],
         compiler_params=PARAMS,
         cost_estimate=cost(0.75),
-    )(owners, ranks, before, own, after, labels, *matrices, *inner)
+    )(owners, ranks, ends, before, own, after, labels, *matrices, *inner)
 
 
 def local(image, labels, brick_blocks, block_owner):
@@ -371,13 +371,16 @@
     owners = jnp.sum(listed * block_owner[None, :], axis=1)
     ranks = jnp.sum(listed * owner_rank[None, :], axis=1)
 
-    matrices = filter_matrices(*labels.shape[1:])
-    left, right = extended(image, "gy", 1, HALO)
-    own = jnp.concatenate([left, image, right], axis=1)
-    before, after = extended(own, "gz", 0, HALO)
-    inner = inner_sums(own, labels, matrices)
+    left, right, (first, last) = neighbours(image, "gy", 1, HALO)
+    zero = jnp.zeros((), image.dtype)
+    own = jnp.concatenate(
+        [jnp.where(first, zero, left), image, jnp.where(last, zero, right)], axis=1
+    )
+    before, after, ends = neighbours(own, "gz", 0, HALO)
+    inner = inner_sums(own, labels)
     likeness, message = outer_sums(
-        owners, ranks, before, own, after, labels, matrices, inner, groups, quarters
+        owners, ranks, jnp.stack(ends).astype(jnp.int32), before, own, after, labels, inner,
+        groups, quarters,
     )
     message = message.reshape(groups * quarters, SEND, LBL)
     got = lax.all_to_all(message, ("gy", "gz"), 0, 0, tiled=True)

time: 90.7 us -> 77.8 us (0.86)
  Pallas kernels: 43.5 us -> 37.5 us
  starting transfers between devices: 12 us -> 6.59 us
  blocking collectives: 27.9 us -> 26.8 us
    ppermute x4, starting transfers between devices: 12 us -> 6.59 us  [the longest x2 3.83 us: neighbours(): lax.ppermute(leading, axis, down)]
    pallas_call x1, Pallas kernels: 11.6 us -> 8.21 us  [inner_sums(): pl.pallas_call(inner_kernel, out_shape=(jax.ShapeDtypeStruct(labels.shape...]
    pallas_call x1, Pallas kernels: 29.6 us -> 27.1 us  [outer_sums(): pl.pallas_call(outer_kernel, out_shape=(jax.ShapeDtypeStruct(labels.shape...]
    all_to_all x1, blocking collectives: 27.9 us -> 26.8 us  [local(): got = lax.all_to_all(message, ('gy', 'gz'), 0, 0, tiled=True)]
  transfers between devices with their start and end apart: 4 -> 4, of which waited for: 1 -> 2; matrix products, arithmetic and copies ran while one was open for 1% -> 1% of each run, Pallas kernels for 13% -> 11%
where the time goes in v3:
time: 77.8 us; the launch traced here: 77.6 us
  Pallas kernels  37.5 us (48%)
  blocking collectives  26.8 us (34%)
  starting transfers between devices  6.59 us (8%)
  waiting for transfers between devices  2.92 us (4%)
  local copies, waits for them, and re-layouts  2.39 us (3%)
    pallas_call x1, Pallas kernels, outer_sums(): pl.pallas_call(outer_kernel, out_shape=(jax.ShapeDtypeStruct(labels.shape...  27.1 us
    all_to_all x1, blocking collectives, local(): got = lax.all_to_all(message, ('gy', 'gz'), 0, 0, tiled=True)  26.8 us
    pallas_call x1, Pallas kernels, inner_sums(): pl.pallas_call(inner_kernel, out_shape=(jax.ShapeDtypeStruct(labels.shape...  8.21 us
    ppermute x2, starting transfers between devices, neighbours(): lax.ppermute(leading, axis, down)  3.83 us
    ppermute x2, starting transfers between devices, neighbours(): lax.ppermute(last, axis, up)  2.76 us
    ppermute x2, waiting for transfers between devices, neighbours(): lax.ppermute(leading, axis, down)  2.72 us
    pallas_call x1, Pallas kernels, local(): pl.pallas_call(sum_kernel, out_shape=jax.ShapeDtypeStruct((blk_dev, FEAT...  2.19 us
  transfers between devices with their start and end apart: 4, of which 2 were waited for; matrix products, arithmetic and copies ran while one was open for 1% of the time, Pallas kernels for 11%

profile of v3, /device:TPU:1, one launch (start us, length us, event | category | flops | bytes accessed | tf_op | source)
XLA Modules:
  0.0 77.6 jit_solution(17627584300725995292)
XLA Ops:
  0.6 1.0 %fusion.2 = (bf16[32,12,128]{2,1,0:T(8,128)(2,1)S(1)}, bf16[32,12,128]{2,1,0:T(8,128)(2,1)S(1)}) fusion(bf16[32,24,128]{2,1,0:T(8,128)(2,1)} %param.10), kind=kLoop, calls=%fused_computation.11 | loop fusion | bytes 393216 | tf_op jit(solution)/shard_map/slice | solution.py:292
  1.7 2.8 %collective-permute-start = (bf16[32,12,128]{2,1,0:T(8,128)(2,1)S(1)}, bf16[32,12,128]{2,1,0:T(8,128)(2,1)S(1)}, u32[]{:S(2)}, u32[]{:S(2)}) collective-permute-start(bf16[32,12,128]{2,1,0:T(8,128)(2,1)S(1)} %get-tuple-element.14), channel_id=1, source_target_pairs={{0,4},{4,8},{8,12},{12,16},{16,20},{20,24},{24,28},{28,32},{32,36}... | collective-permute-start | bytes 294920 | tf_op jit(solution)/shard_map/ppermute | solution.py:296
  4.4 0.0 collective-permute-start.1
  4.4 0.0 copy-start.6
  4.4 0.7 copy-done.6
  5.1 0.2 convert_reduce_fusion
  5.2 0.0 copy-start.7
  5.3 0.7 copy-done.7
  5.9 0.2 select_reduce_fusion
  6.1 0.1 add_convert_fusion.ends_ref
  6.2 0.2 collective-permute-done
  6.4 0.0 copy-start.5
  6.4 2.7 %collective-permute-done.1 = bf16[32,12,128]{2,1,0:T(8,128)(2,1)S(1)} collective-permute-done((bf16[32,12,128]{2,1,0:T(8,128)(2,1)S(1)}, bf16[32,12,128]{2,1,0:T(8,128)(2,1)S(1)}, u32[]{:S(2)}, u32[]{:S(2)}) %collective-permute-start.1) | collective-permute-done | bytes 98336 | tf_op jit(solution)/shard_map/ppermute | solution.py:296
  9.1 0.0 copy-start.2
  9.1 0.0 copy-done.5
  9.1 0.0 copy-start.1
  9.1 0.1 pad_maximum_fusion.own_ref
  9.3 0.0 copy-start
  9.3 0.0 copy-start.4
  9.3 3.8 %collective-permute-start.3 = (bf16[12,48,128]{2,1,0:T(8,128)(2,1)S(1)}, bf16[12,48,128]{2,1,0:T(8,128)(2,1)S(1)}, u32[]{:S(2)}, u32[]{:S(2)}) collective-permute-start(bf16[12,48,128]{2,1,0:T(8,128)(2,1)S(1)} %get-tuple-element.12), channel_id=1, source_target_pairs={{1,0},{2,1},{3,2},{0,3},{5,4},{6,5},{7,6},{4,7},{9,8},{10,9},{11,1... | collective-permute-start | bytes 442376 | tf_op jit(solution)/shard_map/ppermute | solution.py:296
  13.2 0.0 copy-start.3
  13.2 0.0 collective-permute-start.2
  13.2 0.0 copy-done.2
  13.2 0.0 copy-done.1
  13.2 0.0 copy-done
  13.2 0.0 copy-done.4
  13.2 8.2 %shard_map.113 = (bf16[32,24,128]{2,1,0:T(8,128)(2,1)S(1)}, f32[512,256]{1,0:T(8,128)S(1)}) custom-call(bf16[32,48,128]{2,1,0:T(8,128)(2,1)S(1)} %pad_maximum_fusion.own_ref, s32[32,24,128]{2,1,0:T(8,128)S(1)} %copy-done, bf16[768,256]{1,0:T(8,128)(2,1)S(1)} %copy-done.2, bf16[2,80,144]{2,1,0:T(8,128)(2,1)S(1)} %copy-done.4, bf16[6,256,256]{2,1,0:T(8,128)(2,1)S(1)} %copy-done.1), custom_call_target="tpu_custom_call" | custom-call | flops 7000000000 | bytes 1000000 | tf_op jit(solution)/shard_map/pallas_call | solution.py:327
  21.4 0.0 collective-permute-done.3.after_ref
  21.4 0.0 collective-permute-done.2.before_ref
  21.4 0.0 copy-done.3
  21.5 27.1 %shard_map.114 = (bf16[32,24,128]{2,1,0:T(8,128)(2,1)}, bf16[32,4,24,128]{3,2,1,0:T(8,128)(2,1)S(1)}) custom-call(s32[16]{0:T(128)S(1)} %get-tuple-element.11.owner_ref, s32[16]{0:T(128)S(1)} %get-tuple-element.10.rank_ref, s32[2]{0:T(128)S(1)} %add_convert_fusion.ends_ref, bf16[12,48,128]{2,1,0:T(8,128)(2,1)S(1)} %collective-permute-done.2.before_ref, ...), custom_call_target="tpu_custom_call" | custom-call | flops 20999999488 | bytes 3000000 | tf_op jit(solution)/shard_map/pallas_call | solution.py:343
  48.6 26.8 %all_to_all.5.got_ref = bf16[128,24,128]{2,1,0:T(8,128)(2,1)} all-to-all(bf16[128,24,128]{2,1,0:T(8,128)(2,1)S(1)} %bitcast.4), channel_id=1, replica_groups=mesh['gy'=32,'gz'=4] {'gy','gz'}, dimensions={0} | all-to-all | bytes 1572864 | tf_op jit(solution)/shard_map/all_to_all | solution.py:386
  75.4 2.2 %shard_map.115 = f32[4,16,128]{2,1,0:T(8,128)} custom-call(bf16[128,24,128]{2,1,0:T(8,128)(2,1)} %all_to_all.5.got_ref), custom_call_target="tpu_custom_call" | custom-call | tf_op jit(solution)/shard_map/pallas_call | solution.py:387
  (3 shorter events, 0.0 us)
Async XLA Ops:
  1.7 4.7 %collective-permute-start = (bf16[32,12,128]{2,1,0:T(8,128)(2,1)S(1)}, bf16[32,12,128]{2,1,0:T(8,128)(2,1)S(1)}, u32[]{:S(2)}, u32[]{:S(2)}) collective-permute-start(bf16[32,12,128]{2,1,0:T(8,128)(2,1)S(1)} %get-tuple-element.14), channel_id=1, source_target_pairs={{0,4},{4,8},{8,12},{12,16},{16,20},{20,24},{24,28},{28,32},{32,36}... | collective-permute-start | bytes 294920 | tf_op jit(solution)/shard_map/ppermute | solution.py:296
  4.4 4.7 %collective-permute-start.1 = (bf16[32,12,128]{2,1,0:T(8,128)(2,1)S(1)}, bf16[32,12,128]{2,1,0:T(8,128)(2,1)S(1)}, u32[]{:S(2)}, u32[]{:S(2)}) collective-permute-start(bf16[32,12,128]{2,1,0:T(8,128)(2,1)S(1)} %get-tuple-element.15), channel_id=1, source_target_pairs={{4,0},{8,4},{12,8},{16,12},{20,16},{24,20},{28,24},{32,28},{36,32}... | collective-permute-start | bytes 294920 | tf_op jit(solution)/shard_map/ppermute | solution.py:296
  4.4 0.7 copy-start.6
  5.2 0.7 copy-start.7
  6.4 2.8 %copy-start.5 = (bf16[32,24,128]{2,1,0:T(8,128)(2,1)S(1)}, bf16[32,24,128]{2,1,0:T(8,128)(2,1)}, u32[]{:S(2)}) copy-start(bf16[32,24,128]{2,1,0:T(8,128)(2,1)} %param.10) | copy-start | bytes 589828
  9.1 4.1 %copy-start.2 = (bf16[768,256]{1,0:T(8,128)(2,1)S(1)}, bf16[768,256]{1,0:T(8,128)(2,1)}, u32[]{:S(2)}) copy-start(bf16[768,256]{1,0:T(8,128)(2,1)} %constant.27.clone.wz_ref) | copy-start | bytes 1179652
  9.1 4.0 %copy-start.1 = (bf16[6,256,256]{2,1,0:T(8,128)(2,1)S(1)}, bf16[6,256,256]{2,1,0:T(8,128)(2,1)}, u32[]{:S(2)}) copy-start(bf16[6,256,256]{2,1,0:T(8,128)(2,1)} %constant.29.clone.wx_ref) | copy-start | bytes 2359300
  9.3 3.9 %copy-start = (s32[32,24,128]{2,1,0:T(8,128)S(1)}, s32[32,24,128]{2,1,0:T(8,128)}, u32[]{:S(2)}) copy-start(s32[32,24,128]{2,1,0:T(8,128)} %labels_ref.3) | copy-start | bytes 1179652
  9.3 3.9 %copy-start.4 = (bf16[2,80,144]{2,1,0:T(8,128)(2,1)S(1)}, bf16[2,80,144]{2,1,0:T(8,128)(2,1)}, u32[]{:S(2)}) copy-start(bf16[2,80,144]{2,1,0:T(8,128)(2,1)} %constant.28.clone.wy_ref) | copy-start | bytes 138244
  9.3 12.1 %collective-permute-start.3 = (bf16[12,48,128]{2,1,0:T(8,128)(2,1)S(1)}, bf16[12,48,128]{2,1,0:T(8,128)(2,1)S(1)}, u32[]{:S(2)}, u32[]{:S(2)}) collective-permute-start(bf16[12,48,128]{2,1,0:T(8,128)(2,1)S(1)} %get-tuple-element.12), channel_id=1, source_target_pairs={{1,0},{2,1},{3,2},{0,3},{5,4},{6,5},{7,6},{4,7},{9,8},{10,9},{11,1... | collective-permute-start | bytes 442376 | tf_op jit(solution)/shard_map/ppermute | solution.py:296
  13.2 8.3 %copy-start.3 = (bf16[576,240]{1,0:T(8,128)(2,1)S(1)}, bf16[576,240]{1,0:T(8,128)(2,1)}, u32[]{:S(2)}) copy-start(bf16[576,240]{1,0:T(8,128)(2,1)} %constant.30.clone.wz_ref) | copy-start | bytes 829444
  13.2 8.3 %collective-permute-start.2 = (bf16[12,48,128]{2,1,0:T(8,128)(2,1)S(1)}, bf16[12,48,128]{2,1,0:T(8,128)(2,1)S(1)}, u32[]{:S(2)}, u32[]{:S(2)}) collective-permute-start(bf16[12,48,128]{2,1,0:T(8,128)(2,1)S(1)} %get-tuple-element.13), channel_id=1, source_target_pairs={{0,1},{1,2},{2,3},{3,0},{4,5},{5,6},{6,7},{7,4},{8,9},{9,10},{10,1... | collective-permute-start | bytes 442376 | tf_op jit(solution)/shard_map/ppermute | solution.py:296

commit v4 on v3

--- a/solution.py
+++ b/solution.py
@@ -12,8 +12,9 @@
 LBL = 128
 FEAT = 64
 HALO = 12
-ZC_IN, ZC_OUT = (8, 6)
-PLANES_IN, PLANES_OUT = (4, 3)
+ZC_IN, ZC_OUT = (8, 12)
+ZP_IN, ZP_OUT = (8, 6)
+PLANES_IN, PLANES_OUT = (4, 4)
 SIGMAS = (2, 4)
 CENTERS = (-1.5, -0.5, 0.5, 1.5)
 ORDERS = ((2, 0, 0), (0, 2, 0), (0, 0, 2), (1, 1, 0), (1, 0, 1), (0, 1, 1))
@@ -84,33 +85,35 @@
     rows_y, width = like_ref.shape[1:]
     deep = rows_y + 2 * HALO
     rows = chunk * rows_y
-    planes = 6 * chunk
-
-    for pair in range(deep // 16):
-        tiles = [
-            ext[pl.ds(z_start, chunk + 2 * HALO), pl.ds(16 * pair + 8 * half, 8), :]
-            .reshape((chunk + 2 * HALO) * 8, width)
-            .astype(BF16)
-            for half in range(2)
-        ]
-        out = jnp.dot(wz_ref[...], jnp.concatenate(tiles, axis=1), preferred_element_type=F32)
-        out = (out[: planes * 8] + out[planes * 8 :]).reshape(planes, 8, 2 * width)
-        out = jnp.concatenate([out[:, :, :width], out[:, :, width:]], axis=1)
-        high, low = split(out)
-        z_high[:, pl.ds(16 * pair, 16), :] = high
-        z_low[:, pl.ds(16 * pair, 16), :] = low
+    piece = wz_ref.shape[0] // (2 * 6 * 8)
+    planes = 6 * piece
+
+    for first in range(0, chunk, piece):
+        for pair in range(deep // 16):
+            tiles = [
+                ext[pl.ds(z_start + first, piece + 2 * HALO), pl.ds(16 * pair + 8 * half, 8), :]
+                .reshape((piece + 2 * HALO) * 8, width)
+                .astype(BF16)
+                for half in range(2)
+            ]
+            out = jnp.dot(wz_ref[...], jnp.concatenate(tiles, axis=1), preferred_element_type=F32)
+            out = (out[: planes * 8] + out[planes * 8 :]).reshape(planes, 8, 2 * width)
+            out = jnp.concatenate([out[:, :, :width], out[:, :, width:]], axis=1)
+            high, low = split(out.reshape(6, piece, 16, width))
+            z_high[:, pl.ds(first, piece), pl.ds(16 * pair, 16), :] = high
+            z_low[:, pl.ds(first, piece), pl.ds(16 * pair, 16), :] = low
 
     for scale in range(2):
         for order_z in range(3):
             for pair in range(chunk // 2):
                 columns = []
                 for half in range(2):
-                    index = (scale * 3 + order_z) * chunk + 2 * pair + half
+                    index = (scale * 3 + order_z, 2 * pair + half)
                     columns.append(
                         jnp.concatenate([z_high[index], z_low[index], z_high[index]], axis=0)
                     )
                 deep_rows = jnp.concatenate(columns, axis=1)
-                count = wy_ref.shape[1] if order_z == 0 else (48 if order_z == 1 else 32)
+                count = (3 - order_z) * rows_y
                 out = jnp.dot(
                     wy_ref[scale, :count, :], deep_rows, preferred_element_type=F32
                 )
@@ -305,8 +308,8 @@
     deep = rows_y + 2 * HALO
     return [
         pltpu.VMEM((slab_z + 2 * HALO, deep, width), F32),
-        pltpu.VMEM((6 * chunk, deep, width), BF16),
-        pltpu.VMEM((6 * chunk, deep, width), BF16),
+        pltpu.VMEM((6, chunk, deep, width), BF16),
+        pltpu.VMEM((6, chunk, deep, width), BF16),
         pltpu.VMEM((12, rows, width), F32),
         pltpu.VMEM((16 * rows, width), F32),
         pltpu.VMEM((4 * rows, width), F32),
@@ -323,7 +326,7 @@
 
 
 def inner_sums(own, labels):
-    matrices = filter_matrices(ZC_IN, *labels.shape[1:])
+    matrices = filter_matrices(ZP_IN, *labels.shape[1:])
     return pl.pallas_call(
         inner_kernel,
         out_shape=(
@@ -339,7 +342,7 @@
 
 
 def outer_sums(owners, ranks, ends, before, own, after, labels, inner, groups, quarters):
-    matrices = filter_matrices(ZC_OUT, *labels.shape[1:])
+    matrices = filter_matrices(ZP_OUT, *labels.shape[1:])
     return pl.pallas_call(
         outer_kernel,
         out_shape=(
@@ -387,6 +390,7 @@
     label_features = pl.pallas_call(
         sum_kernel,
         out_shape=jax.ShapeDtypeStruct((blk_dev, FEAT // quarters, LBL), F32),
+        compiler_params=pltpu.CompilerParams(vmem_limit_bytes=6 * 1024 * 1024),
     )(got)
     return (likeness, label_features)
 

time: 77.8 us -> 75 us (0.964)
  Pallas kernels: 37.5 us -> 34.9 us
    pallas_call x1, Pallas kernels: 27.1 us -> 25.6 us  [outer_sums(): pl.pallas_call(outer_kernel, out_shape=(jax.ShapeDtypeStruct(labels.shape...]
    pallas_call x1, Pallas kernels: 2.19 us -> 1.06 us  [local(): pl.pallas_call(sum_kernel, out_shape=jax.ShapeDtypeStruct((blk_dev, FEAT...]
where the time goes in v4:
time: 75 us; the launch traced here: 74.8 us
  Pallas kernels  34.9 us (47%)
  blocking collectives  26.7 us (36%)
  starting transfers between devices  6.59 us (9%)
  waiting for transfers between devices  2.92 us (4%)
  local copies, waits for them, and re-layouts  2.39 us (3%)
  between operations  0.76 us (1%)
    all_to_all x1, blocking collectives, local(): got = lax.all_to_all(message, ('gy', 'gz'), 0, 0, tiled=True)  26.7 us
    pallas_call x1, Pallas kernels, outer_sums(): pl.pallas_call(outer_kernel, out_shape=(jax.ShapeDtypeStruct(labels.shape...  25.6 us
    pallas_call x1, Pallas kernels, inner_sums(): pl.pallas_call(inner_kernel, out_shape=(jax.ShapeDtypeStruct(labels.shape...  8.22 us
    ppermute x2, starting transfers between devices, neighbours(): lax.ppermute(leading, axis, down)  3.83 us
    ppermute x2, starting transfers between devices, neighbours(): lax.ppermute(last, axis, up)  2.76 us
    ppermute x2, waiting for transfers between devices, neighbours(): lax.ppermute(leading, axis, down)  2.72 us
  transfers between devices with their start and end apart: 4, of which 2 were waited for; matrix products, arithmetic and copies ran while one was open for 1% of the time, Pallas kernels for 11%

profile of v4, /device:TPU:1, one launch (start us, length us, event | category | flops | bytes accessed | tf_op | source)
XLA Modules:
  0.0 74.8 jit_solution(8596187495227282448)
XLA Ops:
  0.6 1.0 %fusion.2 = (bf16[32,12,128]{2,1,0:T(8,128)(2,1)S(1)}, bf16[32,12,128]{2,1,0:T(8,128)(2,1)S(1)}) fusion(bf16[32,24,128]{2,1,0:T(8,128)(2,1)} %param.10), kind=kLoop, calls=%fused_computation.11 | loop fusion | bytes 393216 | tf_op jit(solution)/shard_map/slice | solution.py:295
  1.7 2.8 %collective-permute-start = (bf16[32,12,128]{2,1,0:T(8,128)(2,1)S(1)}, bf16[32,12,128]{2,1,0:T(8,128)(2,1)S(1)}, u32[]{:S(2)}, u32[]{:S(2)}) collective-permute-start(bf16[32,12,128]{2,1,0:T(8,128)(2,1)S(1)} %get-tuple-element.14), channel_id=1, source_target_pairs={{0,4},{4,8},{8,12},{12,16},{16,20},{20,24},{24,28},{28,32},{32,36}... | collective-permute-start | bytes 294920 | tf_op jit(solution)/shard_map/ppermute | solution.py:299
  4.4 0.0 collective-permute-start.1
  4.4 0.0 copy-start.6
  4.4 0.7 copy-done.6
  5.1 0.2 convert_reduce_fusion
  5.2 0.0 copy-start.7
  5.3 0.7 copy-done.7
  5.9 0.2 select_reduce_fusion
  6.1 0.1 add_convert_fusion.ends_ref
  6.2 0.2 collective-permute-done
  6.4 0.0 copy-start.5
  6.4 2.7 %collective-permute-done.1 = bf16[32,12,128]{2,1,0:T(8,128)(2,1)S(1)} collective-permute-done((bf16[32,12,128]{2,1,0:T(8,128)(2,1)S(1)}, bf16[32,12,128]{2,1,0:T(8,128)(2,1)S(1)}, u32[]{:S(2)}, u32[]{:S(2)}) %collective-permute-start.1) | collective-permute-done | bytes 98336 | tf_op jit(solution)/shard_map/ppermute | solution.py:299
  9.1 0.0 copy-start.2
  9.1 0.0 copy-done.5
  9.1 0.0 copy-start.1
  9.1 0.1 pad_maximum_fusion.own_ref
  9.3 0.0 copy-start
  9.3 0.0 copy-start.4
  9.3 3.8 %collective-permute-start.3 = (bf16[12,48,128]{2,1,0:T(8,128)(2,1)S(1)}, bf16[12,48,128]{2,1,0:T(8,128)(2,1)S(1)}, u32[]{:S(2)}, u32[]{:S(2)}) collective-permute-start(bf16[12,48,128]{2,1,0:T(8,128)(2,1)S(1)} %get-tuple-element.12), channel_id=1, source_target_pairs={{1,0},{2,1},{3,2},{0,3},{5,4},{6,5},{7,6},{4,7},{9,8},{10,9},{11,1... | collective-permute-start | bytes 442376 | tf_op jit(solution)/shard_map/ppermute | solution.py:299
  13.2 0.0 copy-start.3
  13.2 0.0 collective-permute-start.2
  13.2 0.0 copy-done.2
  13.2 0.0 copy-done.1
  13.2 0.0 copy-done
  13.2 0.0 copy-done.4
  13.2 8.2 %shard_map.113 = (bf16[32,24,128]{2,1,0:T(8,128)(2,1)S(1)}, f32[512,256]{1,0:T(8,128)S(1)}) custom-call(bf16[32,48,128]{2,1,0:T(8,128)(2,1)S(1)} %pad_maximum_fusion.own_ref, s32[32,24,128]{2,1,0:T(8,128)S(1)} %copy-done, bf16[768,256]{1,0:T(8,128)(2,1)S(1)} %copy-done.2, bf16[2,80,144]{2,1,0:T(8,128)(2,1)S(1)} %copy-done.4, bf16[6,256,256]{2,1,0:T(8,128)(2,1)S(1)} %copy-done.1), custom_call_target="tpu_custom_call" | custom-call | flops 7000000000 | bytes 1000000 | tf_op jit(solution)/shard_map/pallas_call | solution.py:330
  21.4 0.0 collective-permute-done.3.after_ref
  21.4 0.0 collective-permute-done.2.before_ref
  21.5 0.0 copy-done.3
  21.5 25.6 %shard_map.114 = (bf16[32,24,128]{2,1,0:T(8,128)(2,1)}, bf16[32,4,24,128]{3,2,1,0:T(8,128)(2,1)S(1)}) custom-call(s32[16]{0:T(128)S(1)} %get-tuple-element.11.owner_ref, s32[16]{0:T(128)S(1)} %get-tuple-element.10.rank_ref, s32[2]{0:T(128)S(1)} %add_convert_fusion.ends_ref, bf16[12,48,128]{2,1,0:T(8,128)(2,1)S(1)} %collective-permute-done.2.before_ref, ...), custom_call_target="tpu_custom_call" | custom-call | flops 20999999488 | bytes 3000000 | tf_op jit(solution)/shard_map/pallas_call | solution.py:346
  47.1 26.7 %all_to_all.5.got_ref = bf16[128,24,128]{2,1,0:T(8,128)(2,1)S(1)} all-to-all(bf16[128,24,128]{2,1,0:T(8,128)(2,1)S(1)} %bitcast.4), channel_id=1, replica_groups=mesh['gy'=32,'gz'=4] {'gy','gz'}, dimensions={0} | all-to-all | bytes 1572864 | tf_op jit(solution)/shard_map/all_to_all | solution.py:389
  73.8 1.1 %shard_map.115 = f32[4,16,128]{2,1,0:T(8,128)} custom-call(bf16[128,24,128]{2,1,0:T(8,128)(2,1)S(1)} %all_to_all.5.got_ref), custom_call_target="tpu_custom_call" | custom-call | tf_op jit(solution)/shard_map/pallas_call | solution.py:390
  (3 shorter events, 0.0 us)
Async XLA Ops:
  1.7 4.7 %collective-permute-start = (bf16[32,12,128]{2,1,0:T(8,128)(2,1)S(1)}, bf16[32,12,128]{2,1,0:T(8,128)(2,1)S(1)}, u32[]{:S(2)}, u32[]{:S(2)}) collective-permute-start(bf16[32,12,128]{2,1,0:T(8,128)(2,1)S(1)} %get-tuple-element.14), channel_id=1, source_target_pairs={{0,4},{4,8},{8,12},{12,16},{16,20},{20,24},{24,28},{28,32},{32,36}... | collective-permute-start | bytes 294920 | tf_op jit(solution)/shard_map/ppermute | solution.py:299
  4.4 4.7 %collective-permute-start.1 = (bf16[32,12,128]{2,1,0:T(8,128)(2,1)S(1)}, bf16[32,12,128]{2,1,0:T(8,128)(2,1)S(1)}, u32[]{:S(2)}, u32[]{:S(2)}) collective-permute-start(bf16[32,12,128]{2,1,0:T(8,128)(2,1)S(1)} %get-tuple-element.15), channel_id=1, source_target_pairs={{4,0},{8,4},{12,8},{16,12},{20,16},{24,20},{28,24},{32,28},{36,32}... | collective-permute-start | bytes 294920 | tf_op jit(solution)/shard_map/ppermute | solution.py:299
  4.4 0.7 copy-start.6
  5.2 0.7 copy-start.7
  6.4 2.8 %copy-start.5 = (bf16[32,24,128]{2,1,0:T(8,128)(2,1)S(1)}, bf16[32,24,128]{2,1,0:T(8,128)(2,1)}, u32[]{:S(2)}) copy-start(bf16[32,24,128]{2,1,0:T(8,128)(2,1)} %param.10) | copy-start | bytes 589828
  9.1 4.1 %copy-start.2 = (bf16[768,256]{1,0:T(8,128)(2,1)S(1)}, bf16[768,256]{1,0:T(8,128)(2,1)}, u32[]{:S(2)}) copy-start(bf16[768,256]{1,0:T(8,128)(2,1)} %constant.27.clone.wz_ref) | copy-start | bytes 1179652
  9.1 4.0 %copy-start.1 = (bf16[6,256,256]{2,1,0:T(8,128)(2,1)S(1)}, bf16[6,256,256]{2,1,0:T(8,128)(2,1)}, u32[]{:S(2)}) copy-start(bf16[6,256,256]{2,1,0:T(8,128)(2,1)} %constant.29.clone.wx_ref) | copy-start | bytes 2359300
  9.3 3.9 %copy-start = (s32[32,24,128]{2,1,0:T(8,128)S(1)}, s32[32,24,128]{2,1,0:T(8,128)}, u32[]{:S(2)}) copy-start(s32[32,24,128]{2,1,0:T(8,128)} %labels_ref.3) | copy-start | bytes 1179652
  9.3 3.9 %copy-start.4 = (bf16[2,80,144]{2,1,0:T(8,128)(2,1)S(1)}, bf16[2,80,144]{2,1,0:T(8,128)(2,1)}, u32[]{:S(2)}) copy-start(bf16[2,80,144]{2,1,0:T(8,128)(2,1)} %constant.28.clone.wy_ref) | copy-start | bytes 138244
  9.3 12.1 %collective-permute-start.3 = (bf16[12,48,128]{2,1,0:T(8,128)(2,1)S(1)}, bf16[12,48,128]{2,1,0:T(8,128)(2,1)S(1)}, u32[]{:S(2)}, u32[]{:S(2)}) collective-permute-start(bf16[12,48,128]{2,1,0:T(8,128)(2,1)S(1)} %get-tuple-element.12), channel_id=1, source_target_pairs={{1,0},{2,1},{3,2},{0,3},{5,4},{6,5},{7,6},{4,7},{9,8},{10,9},{11,1... | collective-permute-start | bytes 442376 | tf_op jit(solution)/shard_map/ppermute | solution.py:299
  13.2 8.3 %copy-start.3 = (bf16[576,240]{1,0:T(8,128)(2,1)S(1)}, bf16[576,240]{1,0:T(8,128)(2,1)}, u32[]{:S(2)}) copy-start(bf16[576,240]{1,0:T(8,128)(2,1)} %constant.30.clone.wz_ref) | copy-start | bytes 829444
  13.2 8.3 %collective-permute-start.2 = (bf16[12,48,128]{2,1,0:T(8,128)(2,1)S(1)}, bf16[12,48,128]{2,1,0:T(8,128)(2,1)S(1)}, u32[]{:S(2)}, u32[]{:S(2)}) collective-permute-start(bf16[12,48,128]{2,1,0:T(8,128)(2,1)S(1)} %get-tuple-element.13), channel_id=1, source_target_pairs={{0,1},{1,2},{2,3},{3,0},{4,5},{5,6},{6,7},{7,4},{8,9},{9,10},{10,1... | collective-permute-start | bytes 442376 | tf_op jit(solution)/shard_map/ppermute | solution.py:299

commit v5 on v4

--- a/solution.py
+++ b/solution.py
@@ -14,7 +14,7 @@
 HALO = 12
 ZC_IN, ZC_OUT = (8, 12)
 ZP_IN, ZP_OUT = (8, 6)
-PLANES_IN, PLANES_OUT = (4, 4)
+PLANES_IN, PLANES_OUT = (4, 6)
 SIGMAS = (2, 4)
 CENTERS = (-1.5, -0.5, 0.5, 1.5)
 ORDERS = ((2, 0, 0), (0, 2, 0), (0, 0, 2), (1, 1, 0), (1, 0, 1), (0, 1, 1))
@@ -201,10 +201,14 @@
     lax.fori_loop(0, chunk // planes, step, 0)
 
 
-def all_chunks(start_of, count, chunk, planes, ext, labels_ref, weights, passes, buffers, acc, like_ref):
+def all_chunks(
+    start_of, count, chunk, planes, ext, labels_ref, weights, passes, buffers, acc, like_ref,
+    beside=lambda index: None,
+):
     def step(index, carry):
         z_start = start_of(index)
         filters_of(z_start, chunk, ext, *weights, *passes, *buffers, like_ref)
+        beside(index)
         add_sums(z_start, chunk, planes, labels_ref, *buffers, acc)
         return carry
 
@@ -230,7 +234,7 @@
     owner_ref, rank_ref, ends_ref, before_ref, own_ref, after_ref, labels_ref, wz_ref, wy_ref,
     wx_ref, inner_like_ref, inner_acc_ref,
     like_ref, send_ref,
-    ext, z_high, z_low, y_out, channels, bands, acc, turned,
+    ext, z_high, z_low, y_out, channels, bands, acc, turned, like, like_sems,
 ):
     slab_z = labels_ref.shape[0]
     ext[pl.ds(HALO, slab_z)] = own_ref[...].astype(F32)
@@ -238,19 +242,31 @@
         ext[pl.ds(at, HALO)] = jnp.where(ends_ref[end] != 0, 0.0, ref[...].astype(F32))
     acc[...] = inner_acc_ref[...]
     inner = pl.ds(HALO, slab_z - 2 * HALO)
-    like_ref[inner] = inner_like_ref[inner]
     half = HALO // ZC_OUT
+    count = 2 * half
+    share = send_ref.shape[0] // count
+    inner_copy = pltpu.make_async_copy(
+        inner_like_ref.at[inner], like_ref.at[inner], like_sems.at[count]
+    )
+    inner_copy.start()
 
     def start_of(index):
         return index * ZC_OUT + jnp.where(index >= half, slab_z - 2 * HALO, 0)
 
+    def like_copy(index):
+        planes = pl.ds(start_of(index), ZC_OUT)
+        return pltpu.make_async_copy(like.at[planes], like_ref.at[planes], like_sems.at[index])
+
+    def beside(index):
+        send_ref[pl.ds(index * share, share)] = jnp.zeros((share, *send_ref.shape[1:]), BF16)
+        like_copy(index).start()
+
     all_chunks(
-        start_of, 2 * half, ZC_OUT, PLANES_OUT, ext, labels_ref,
+        start_of, count, ZC_OUT, PLANES_OUT, ext, labels_ref,
         (wz_ref, wy_ref, wx_ref), (z_high, z_low, y_out),
-        (channels, bands), acc, like_ref,
-    )
-
-    send_ref[...] = jnp.zeros_like(send_ref)
+        (channels, bands), acc, like, beside,
+    )
+
     for slot in range(owner_ref.shape[0]):
         owner = owner_ref[slot]
         rank = rank_ref[slot].astype(F32)
@@ -265,6 +281,9 @@
                 BF16
             )
             send_ref[owner, quarter, pl.ds(16, 8), :] = jnp.full((8, LBL), rank, F32).astype(BF16)
+    for index in range(count):
+        like_copy(index).wait()
+    inner_copy.wait()
 
 
 def sum_kernel(got_ref, out_ref):
@@ -350,9 +369,14 @@
             jax.ShapeDtypeStruct((groups, quarters, SEND, LBL), BF16),
         ),
         in_specs=[SMEM] * 3 + [VMEM] * 9,
-        out_specs=(VMEM, VMEM),
+        out_specs=(pl.BlockSpec(memory_space=pl.ANY), VMEM),
         scratch_shapes=scratch(ZC_OUT, *labels.shape)
-        + [pltpu.VMEM((HI * FEAT, LO), F32), pltpu.VMEM((FEAT, LBL), F32)],
+        + [
+            pltpu.VMEM((HI * FEAT, LO), F32),
+            pltpu.VMEM((FEAT, LBL), F32),
+            pltpu.VMEM(labels.shape, BF16),
+            pltpu.SemaphoreType.DMA((2 * HALO // ZC_OUT + 1,)),
+        ],
         compiler_params=PARAMS,
         cost_estimate=cost(0.75),
     )(owners, ranks, ends, before, own, after, labels, *matrices, *inner)

time: 75 us -> 74.1 us (0.988)
  Pallas kernels: 34.9 us -> 33.9 us
    pallas_call x1, Pallas kernels: 25.6 us -> 24.6 us  [outer_sums(): pl.pallas_call(outer_kernel, out_shape=(jax.ShapeDtypeStruct(labels.shape...]
where the time goes in v5:
time: 74.1 us; the launch traced here: 73.9 us
  Pallas kernels  33.9 us (46%)
  blocking collectives  26.7 us (36%)
  starting transfers between devices  6.59 us (9%)
  waiting for transfers between devices  2.92 us (4%)
  local copies, waits for them, and re-layouts  2.39 us (3%)
  between operations  0.77 us (1%)
    all_to_all x1, blocking collectives, local(): got = lax.all_to_all(message, ('gy', 'gz'), 0, 0, tiled=True)  26.7 us
    pallas_call x1, Pallas kernels, outer_sums(): pl.pallas_call(outer_kernel, out_shape=(jax.ShapeDtypeStruct(labels.shape...  24.6 us
    pallas_call x1, Pallas kernels, inner_sums(): pl.pallas_call(inner_kernel, out_shape=(jax.ShapeDtypeStruct(labels.shape...  8.22 us
    ppermute x2, starting transfers between devices, neighbours(): lax.ppermute(leading, axis, down)  3.83 us
    ppermute x2, starting transfers between devices, neighbours(): lax.ppermute(last, axis, up)  2.76 us
    ppermute x2, waiting for transfers between devices, neighbours(): lax.ppermute(leading, axis, down)  2.72 us
  transfers between devices with their start and end apart: 4, of which 2 were waited for; matrix products, arithmetic and copies ran while one was open for 1% of the time, Pallas kernels for 11%

profile of v5, /device:TPU:1, one launch (start us, length us, event | category | flops | bytes accessed | tf_op | source)
XLA Modules:
  0.0 73.9 jit_solution(6427953158496434988)
XLA Ops:
  0.6 1.0 %fusion.2 = (bf16[32,12,128]{2,1,0:T(8,128)(2,1)S(1)}, bf16[32,12,128]{2,1,0:T(8,128)(2,1)S(1)}) fusion(bf16[32,24,128]{2,1,0:T(8,128)(2,1)} %param.10), kind=kLoop, calls=%fused_computation.11 | loop fusion | bytes 393216 | tf_op jit(solution)/shard_map/slice | solution.py:314
  1.7 2.8 %collective-permute-start = (bf16[32,12,128]{2,1,0:T(8,128)(2,1)S(1)}, bf16[32,12,128]{2,1,0:T(8,128)(2,1)S(1)}, u32[]{:S(2)}, u32[]{:S(2)}) collective-permute-start(bf16[32,12,128]{2,1,0:T(8,128)(2,1)S(1)} %get-tuple-element.14), channel_id=1, source_target_pairs={{0,4},{4,8},{8,12},{12,16},{16,20},{20,24},{24,28},{28,32},{32,36}... | collective-permute-start | bytes 294920 | tf_op jit(solution)/shard_map/ppermute | solution.py:318
  4.4 0.0 collective-permute-start.1
  4.4 0.0 copy-start.6
  4.4 0.7 copy-done.6
  5.1 0.2 convert_reduce_fusion
  5.2 0.0 copy-start.7
  5.3 0.7 copy-done.7
  5.9 0.2 select_reduce_fusion
  6.1 0.1 add_convert_fusion.ends_ref
  6.2 0.2 collective-permute-done
  6.4 0.0 copy-start.5
  6.4 2.7 %collective-permute-done.1 = bf16[32,12,128]{2,1,0:T(8,128)(2,1)S(1)} collective-permute-done((bf16[32,12,128]{2,1,0:T(8,128)(2,1)S(1)}, bf16[32,12,128]{2,1,0:T(8,128)(2,1)S(1)}, u32[]{:S(2)}, u32[]{:S(2)}) %collective-permute-start.1) | collective-permute-done | bytes 98336 | tf_op jit(solution)/shard_map/ppermute | solution.py:318
  9.1 0.0 copy-start.2
  9.1 0.0 copy-done.5
  9.1 0.0 copy-start.1
  9.1 0.1 pad_maximum_fusion.own_ref
  9.3 0.0 copy-start
  9.3 0.0 copy-start.4
  9.3 3.8 %collective-permute-start.3 = (bf16[12,48,128]{2,1,0:T(8,128)(2,1)S(1)}, bf16[12,48,128]{2,1,0:T(8,128)(2,1)S(1)}, u32[]{:S(2)}, u32[]{:S(2)}) collective-permute-start(bf16[12,48,128]{2,1,0:T(8,128)(2,1)S(1)} %get-tuple-element.12), channel_id=1, source_target_pairs={{1,0},{2,1},{3,2},{0,3},{5,4},{6,5},{7,6},{4,7},{9,8},{10,9},{11,1... | collective-permute-start | bytes 442376 | tf_op jit(solution)/shard_map/ppermute | solution.py:318
  13.2 0.0 copy-start.3
  13.2 0.0 collective-permute-start.2
  13.2 0.0 copy-done.2
  13.2 0.0 copy-done.1
  13.2 0.0 copy-done
  13.2 0.0 copy-done.4
  13.2 8.2 %shard_map.113 = (bf16[32,24,128]{2,1,0:T(8,128)(2,1)S(1)}, f32[512,256]{1,0:T(8,128)S(1)}) custom-call(bf16[32,48,128]{2,1,0:T(8,128)(2,1)S(1)} %pad_maximum_fusion.own_ref, s32[32,24,128]{2,1,0:T(8,128)S(1)} %copy-done, bf16[768,256]{1,0:T(8,128)(2,1)S(1)} %copy-done.2, bf16[2,80,144]{2,1,0:T(8,128)(2,1)S(1)} %copy-done.4, bf16[6,256,256]{2,1,0:T(8,128)(2,1)S(1)} %copy-done.1), custom_call_target="tpu_custom_call" | custom-call | flops 7000000000 | bytes 1000000 | tf_op jit(solution)/shard_map/pallas_call | solution.py:349
  21.4 0.0 collective-permute-done.3.after_ref
  21.4 0.0 collective-permute-done.2.before_ref
  21.5 0.0 copy-done.3
  21.5 24.6 %shard_map.114 = (bf16[32,24,128]{2,1,0:T(8,128)(2,1)}, bf16[32,4,24,128]{3,2,1,0:T(8,128)(2,1)S(1)}) custom-call(s32[16]{0:T(128)S(1)} %get-tuple-element.11.owner_ref, s32[16]{0:T(128)S(1)} %get-tuple-element.10.rank_ref, s32[2]{0:T(128)S(1)} %add_convert_fusion.ends_ref, bf16[12,48,128]{2,1,0:T(8,128)(2,1)S(1)} %collective-permute-done.2.before_ref, ...), custom_call_target="tpu_custom_call" | custom-call | flops 20999999488 | bytes 3000000 | tf_op jit(solution)/shard_map/pallas_call | solution.py:365
  46.1 26.7 %all_to_all.5.got_ref = bf16[128,24,128]{2,1,0:T(8,128)(2,1)S(1)} all-to-all(bf16[128,24,128]{2,1,0:T(8,128)(2,1)S(1)} %bitcast.4), channel_id=1, replica_groups=mesh['gy'=32,'gz'=4] {'gy','gz'}, dimensions={0} | all-to-all | bytes 1572864 | tf_op jit(solution)/shard_map/all_to_all | solution.py:413
  72.8 1.1 %shard_map.115 = f32[4,16,128]{2,1,0:T(8,128)} custom-call(bf16[128,24,128]{2,1,0:T(8,128)(2,1)S(1)} %all_to_all.5.got_ref), custom_call_target="tpu_custom_call" | custom-call | tf_op jit(solution)/shard_map/pallas_call | solution.py:414
  (3 shorter events, 0.0 us)
Async XLA Ops:
  1.7 4.7 %collective-permute-start = (bf16[32,12,128]{2,1,0:T(8,128)(2,1)S(1)}, bf16[32,12,128]{2,1,0:T(8,128)(2,1)S(1)}, u32[]{:S(2)}, u32[]{:S(2)}) collective-permute-start(bf16[32,12,128]{2,1,0:T(8,128)(2,1)S(1)} %get-tuple-element.14), channel_id=1, source_target_pairs={{0,4},{4,8},{8,12},{12,16},{16,20},{20,24},{24,28},{28,32},{32,36}... | collective-permute-start | bytes 294920 | tf_op jit(solution)/shard_map/ppermute | solution.py:318
  4.4 4.7 %collective-permute-start.1 = (bf16[32,12,128]{2,1,0:T(8,128)(2,1)S(1)}, bf16[32,12,128]{2,1,0:T(8,128)(2,1)S(1)}, u32[]{:S(2)}, u32[]{:S(2)}) collective-permute-start(bf16[32,12,128]{2,1,0:T(8,128)(2,1)S(1)} %get-tuple-element.15), channel_id=1, source_target_pairs={{4,0},{8,4},{12,8},{16,12},{20,16},{24,20},{28,24},{32,28},{36,32}... | collective-permute-start | bytes 294920 | tf_op jit(solution)/shard_map/ppermute | solution.py:318
  4.4 0.7 copy-start.6
  5.2 0.7 copy-start.7
  6.4 2.8 %copy-start.5 = (bf16[32,24,128]{2,1,0:T(8,128)(2,1)S(1)}, bf16[32,24,128]{2,1,0:T(8,128)(2,1)}, u32[]{:S(2)}) copy-start(bf16[32,24,128]{2,1,0:T(8,128)(2,1)} %param.10) | copy-start | bytes 589828
  9.1 4.1 %copy-start.2 = (bf16[768,256]{1,0:T(8,128)(2,1)S(1)}, bf16[768,256]{1,0:T(8,128)(2,1)}, u32[]{:S(2)}) copy-start(bf16[768,256]{1,0:T(8,128)(2,1)} %constant.27.clone.wz_ref) | copy-start | bytes 1179652
  9.1 4.0 %copy-start.1 = (bf16[6,256,256]{2,1,0:T(8,128)(2,1)S(1)}, bf16[6,256,256]{2,1,0:T(8,128)(2,1)}, u32[]{:S(2)}) copy-start(bf16[6,256,256]{2,1,0:T(8,128)(2,1)} %constant.29.clone.wx_ref) | copy-start | bytes 2359300
  9.3 3.9 %copy-start = (s32[32,24,128]{2,1,0:T(8,128)S(1)}, s32[32,24,128]{2,1,0:T(8,128)}, u32[]{:S(2)}) copy-start(s32[32,24,128]{2,1,0:T(8,128)} %labels_ref.3) | copy-start | bytes 1179652
  9.3 3.9 %copy-start.4 = (bf16[2,80,144]{2,1,0:T(8,128)(2,1)S(1)}, bf16[2,80,144]{2,1,0:T(8,128)(2,1)}, u32[]{:S(2)}) copy-start(bf16[2,80,144]{2,1,0:T(8,128)(2,1)} %constant.28.clone.wy_ref) | copy-start | bytes 138244
  9.3 12.1 %collective-permute-start.3 = (bf16[12,48,128]{2,1,0:T(8,128)(2,1)S(1)}, bf16[12,48,128]{2,1,0:T(8,128)(2,1)S(1)}, u32[]{:S(2)}, u32[]{:S(2)}) collective-permute-start(bf16[12,48,128]{2,1,0:T(8,128)(2,1)S(1)} %get-tuple-element.12), channel_id=1, source_target_pairs={{1,0},{2,1},{3,2},{0,3},{5,4},{6,5},{7,6},{4,7},{9,8},{10,9},{11,1... | collective-permute-start | bytes 442376 | tf_op jit(solution)/shard_map/ppermute | solution.py:318
  13.2 8.3 %copy-start.3 = (bf16[576,240]{1,0:T(8,128)(2,1)S(1)}, bf16[576,240]{1,0:T(8,128)(2,1)}, u32[]{:S(2)}) copy-start(bf16[576,240]{1,0:T(8,128)(2,1)} %constant.30.clone.wz_ref) | copy-start | bytes 829444
  13.2 8.3 %collective-permute-start.2 = (bf16[12,48,128]{2,1,0:T(8,128)(2,1)S(1)}, bf16[12,48,128]{2,1,0:T(8,128)(2,1)S(1)}, u32[]{:S(2)}, u32[]{:S(2)}) collective-permute-start(bf16[12,48,128]{2,1,0:T(8,128)(2,1)S(1)} %get-tuple-element.13), channel_id=1, source_target_pairs={{0,1},{1,2},{2,3},{3,0},{4,5},{5,6},{6,7},{7,4},{8,9},{9,10},{10,1... | collective-permute-start | bytes 442376 | tf_op jit(solution)/shard_map/ppermute | solution.py:318

commit v6 on v5

--- a/solution.py
+++ b/solution.py
@@ -318,6 +318,21 @@
     return (lax.ppermute(last, axis, up), lax.ppermute(leading, axis, down), ends)
 
 
+def paired_neighbours(shard, axis, dim, width):
+    size, length = (lax.axis_size(axis), shard.shape[dim])
+    here = lax.axis_index(axis)
+    odd = here % 2 == 1
+    last = lax.slice_in_dim(shard, length - width, length, axis=dim)
+    leading = lax.slice_in_dim(shard, 0, width, axis=dim)
+    outer = [(i, (i + 1) % size if i % 2 else (i - 1) % size) for i in range(size)]
+    inner = [(i, i ^ 1) for i in range(size)]
+    from_outer = lax.ppermute(jnp.where(odd, last, leading), axis, outer)
+    from_inner = lax.ppermute(jnp.where(odd, leading, last), axis, inner)
+    before = jnp.where(odd, from_inner, from_outer)
+    after = jnp.where(odd, from_outer, from_inner)
+    return (before, after, (here == 0, here == size - 1))
+
+
 VMEM = pl.BlockSpec(memory_space=pltpu.VMEM)
 SMEM = pl.BlockSpec(memory_space=pltpu.SMEM)
 
@@ -398,7 +413,7 @@
     owners = jnp.sum(listed * block_owner[None, :], axis=1)
     ranks = jnp.sum(listed * owner_rank[None, :], axis=1)
 
-    left, right, (first, last) = neighbours(image, "gy", 1, HALO)
+    left, right, (first, last) = paired_neighbours(image, "gy", 1, HALO)
     zero = jnp.zeros((), image.dtype)
     own = jnp.concatenate(
         [jnp.where(first, zero, left), image, jnp.where(last, zero, right)], axis=1

time: 74.1 us -> 74.4 us (level)
  blocking collectives: 26.7 us -> 28.5 us
  waiting for transfers between devices: 2.92 us -> 1.29 us
  local copies, waits for them, and re-layouts: 2.39 us -> 1.36 us
  other arithmetic: 0.59 us -> 1.61 us
    ppermute x0 -> x2, starting transfers between devices: none -> 2.86 us  [the longest x1 1.5 us: paired_neighbours(): from_inner = lax.ppermute(jnp.where(odd, leading, last), axis, inner)]
    ppermute x2 -> x1, starting transfers between devices: 2.76 us -> 0.01 us  [neighbours(): lax.ppermute(last, axis, up)]
    ppermute x2 -> x1, waiting for transfers between devices: 2.72 us -> 0.01 us  [neighbours(): lax.ppermute(leading, axis, down)]
    all_to_all x1, blocking collectives: 26.7 us -> 28.5 us  [local(): got = lax.all_to_all(message, ('gy', 'gz'), 0, 0, tiled=True)]
    ppermute x0 -> x2, waiting for transfers between devices: none -> 1.28 us  [the longest x1 1.28 us: paired_neighbours(): from_outer = lax.ppermute(jnp.where(odd, last, leading), axis, outer)]
    slice x1 -> x0, local copies, waits for them, and re-layouts: 1.03 us -> none  [neighbours(): last = lax.slice_in_dim(shard, length - width, length, axis=dim)]
    select_n x1, other arithmetic: 0.01 us -> 1.03 us  [paired_neighbours(): from_inner = lax.ppermute(jnp.where(odd, leading, last), axis, inner)]
    ppermute x2 -> x1, starting transfers between devices: 3.83 us -> 3.91 us  [neighbours(): lax.ppermute(leading, axis, down)]
  transfers between devices with their start and end apart: 4 -> 4, of which waited for: 2 -> 1; matrix products, arithmetic and copies ran while one was open for 1% -> 1% of each run, Pallas kernels for 11% -> 11%
where the time goes in v6:
time: 74.4 us; the launch traced here: 74.2 us
  Pallas kernels  33.9 us (46%)
  blocking collectives  28.5 us (38%)
  starting transfers between devices  6.77 us (9%)
  other arithmetic  1.61 us (2%)
  local copies, waits for them, and re-layouts  1.36 us (2%)
  waiting for transfers between devices  1.29 us (2%)
  between operations  0.78 us (1%)
    all_to_all x1, blocking collectives, local(): got = lax.all_to_all(message, ('gy', 'gz'), 0, 0, tiled=True)  28.5 us
    pallas_call x1, Pallas kernels, outer_sums(): pl.pallas_call(outer_kernel, out_shape=(jax.ShapeDtypeStruct(labels.shape...  24.6 us
    pallas_call x1, Pallas kernels, inner_sums(): pl.pallas_call(inner_kernel, out_shape=(jax.ShapeDtypeStruct(labels.shape...  8.22 us
    ppermute x1, starting transfers between devices, neighbours(): lax.ppermute(leading, axis, down)  3.91 us
    ppermute x1, starting transfers between devices, paired_neighbours(): from_inner = lax.ppermute(jnp.where(odd, leading, last), axis, inner)  1.5 us
  transfers between devices with their start and end apart: 4, of which 1 were waited for; matrix products, arithmetic and copies ran while one was open for 1% of the time, Pallas kernels for 11%

profile of v6, /device:TPU:1, one launch (start us, length us, event | category | flops | bytes accessed | tf_op | source)
XLA Modules:
  0.0 74.2 jit_solution(16956966162399487061)
XLA Ops:
  0.6 1.0 %broadcast_select_fusion.1 = (bf16[32,12,128]{2,1,0:T(8,128)(2,1)S(1)}, bf16[32,12,128]{2,1,0:T(8,128)(2,1)S(1)}) fusion(pred[]{:T(512)S(6)} %eq.55, bf16[32,24,128]{2,1,0:T(8,128)(2,1)} %param.10), kind=kLoop, calls=%fused_computation.4 | loop fusion | flops 98304 | bytes 393217 | tf_op jit(solution)/shard_map/jit(_where)/select_n | solution.py:330
  1.7 1.5 %collective-permute-start = (bf16[32,12,128]{2,1,0:T(8,128)(2,1)S(1)}, bf16[32,12,128]{2,1,0:T(8,128)(2,1)S(1)}, u32[]{:S(2)}, u32[]{:S(2)}) collective-permute-start(bf16[32,12,128]{2,1,0:T(8,128)(2,1)S(1)} %get-tuple-element.16), channel_id=1, source_target_pairs={{0,4},{4,0},{8,12},{12,8},{16,20},{20,16},{24,28},{28,24},{32,36},... | collective-permute-start | bytes 294920 | tf_op jit(solution)/shard_map/ppermute | solution.py:330
  3.2 1.4 %collective-permute-start.1 = (bf16[32,12,128]{2,1,0:T(8,128)(2,1)S(1)}, bf16[32,12,128]{2,1,0:T(8,128)(2,1)S(1)}, u32[]{:S(2)}, u32[]{:S(2)}) collective-permute-start(bf16[32,12,128]{2,1,0:T(8,128)(2,1)S(1)} %get-tuple-element.17), channel_id=1, source_target_pairs={{0,124},{4,8},{8,4},{12,16},{16,12},{20,24},{24,20},{28,32},{32,28... | collective-permute-start | bytes 294920 | tf_op jit(solution)/shard_map/ppermute | solution.py:329
  4.5 0.0 copy-start.6
  4.5 0.7 copy-done.6
  5.2 0.2 convert_reduce_fusion
  5.4 0.0 copy-start.7
  5.4 0.7 copy-done.7
  6.0 0.2 select_reduce_fusion
  6.2 0.1 add_convert_fusion.ends_ref
  6.3 0.0 copy-start.5
  6.3 0.0 collective-permute-done
  6.3 1.3 %collective-permute-done.1 = bf16[32,12,128]{2,1,0:T(8,128)(2,1)S(1)} collective-permute-done((bf16[32,12,128]{2,1,0:T(8,128)(2,1)S(1)}, bf16[32,12,128]{2,1,0:T(8,128)(2,1)S(1)}, u32[]{:S(2)}, u32[]{:S(2)}) %collective-permute-start.1) | collective-permute-done | bytes 98336 | tf_op jit(solution)/shard_map/ppermute | solution.py:329
  7.6 0.0 copy-start.2
  7.6 0.0 copy-start.1
  7.6 0.0 copy-done.5
  7.6 0.1 pad_maximum_fusion.own_ref
  7.8 0.0 copy-start
  7.8 0.0 copy-start.4
  7.8 3.9 %collective-permute-start.3 = (bf16[12,48,128]{2,1,0:T(8,128)(2,1)S(1)}, bf16[12,48,128]{2,1,0:T(8,128)(2,1)S(1)}, u32[]{:S(2)}, u32[]{:S(2)}) collective-permute-start(bf16[12,48,128]{2,1,0:T(8,128)(2,1)S(1)} %get-tuple-element.12), channel_id=1, source_target_pairs={{1,0},{2,1},{3,2},{0,3},{5,4},{6,5},{7,6},{4,7},{9,8},{10,9},{11,1... | collective-permute-start | bytes 442376 | tf_op jit(solution)/shard_map/ppermute | solution.py:318
  11.7 0.0 copy-start.3
  11.7 0.0 collective-permute-start.2
  11.7 0.0 copy-done.2
  11.7 0.0 copy-done.1
  11.7 0.0 copy-done
  11.8 0.0 copy-done.4
  11.8 8.2 %shard_map.113 = (bf16[32,24,128]{2,1,0:T(8,128)(2,1)S(1)}, f32[512,256]{1,0:T(8,128)S(1)}) custom-call(bf16[32,48,128]{2,1,0:T(8,128)(2,1)S(1)} %pad_maximum_fusion.own_ref, s32[32,24,128]{2,1,0:T(8,128)S(1)} %copy-done, bf16[768,256]{1,0:T(8,128)(2,1)S(1)} %copy-done.2, bf16[2,80,144]{2,1,0:T(8,128)(2,1)S(1)} %copy-done.4, bf16[6,256,256]{2,1,0:T(8,128)(2,1)S(1)} %copy-done.1), custom_call_target="tpu_custom_call" | custom-call | flops 7000000000 | bytes 1000000 | tf_op jit(solution)/shard_map/pallas_call | solution.py:364
  20.0 0.0 collective-permute-done.3.after_ref
  20.0 0.0 collective-permute-done.2.before_ref
  20.0 0.0 copy-done.3
  20.0 24.6 %shard_map.114 = (bf16[32,24,128]{2,1,0:T(8,128)(2,1)}, bf16[32,4,24,128]{3,2,1,0:T(8,128)(2,1)S(1)}) custom-call(s32[16]{0:T(128)S(1)} %get-tuple-element.11.owner_ref, s32[16]{0:T(128)S(1)} %get-tuple-element.10.rank_ref, s32[2]{0:T(128)S(1)} %add_convert_fusion.ends_ref, bf16[12,48,128]{2,1,0:T(8,128)(2,1)S(1)} %collective-permute-done.2.before_ref, ...), custom_call_target="tpu_custom_call" | custom-call | flops 20999999488 | bytes 3000000 | tf_op jit(solution)/shard_map/pallas_call | solution.py:380
  44.7 28.5 %all_to_all.5.got_ref = bf16[128,24,128]{2,1,0:T(8,128)(2,1)S(1)} all-to-all(bf16[128,24,128]{2,1,0:T(8,128)(2,1)S(1)} %bitcast.4), channel_id=1, replica_groups=mesh['gy'=32,'gz'=4] {'gy','gz'}, dimensions={0} | all-to-all | bytes 1572864 | tf_op jit(solution)/shard_map/all_to_all | solution.py:428
  73.1 1.1 %shard_map.115 = f32[4,16,128]{2,1,0:T(8,128)} custom-call(bf16[128,24,128]{2,1,0:T(8,128)(2,1)S(1)} %all_to_all.5.got_ref), custom_call_target="tpu_custom_call" | custom-call | tf_op jit(solution)/shard_map/pallas_call | solution.py:429
  (2 shorter events, 0.0 us)
Async XLA Ops:
  1.7 4.6 %collective-permute-start = (bf16[32,12,128]{2,1,0:T(8,128)(2,1)S(1)}, bf16[32,12,128]{2,1,0:T(8,128)(2,1)S(1)}, u32[]{:S(2)}, u32[]{:S(2)}) collective-permute-start(bf16[32,12,128]{2,1,0:T(8,128)(2,1)S(1)} %get-tuple-element.16), channel_id=1, source_target_pairs={{0,4},{4,0},{8,12},{12,8},{16,20},{20,16},{24,28},{28,24},{32,36},... | collective-permute-start | bytes 294920 | tf_op jit(solution)/shard_map/ppermute | solution.py:330
  3.2 4.4 %collective-permute-start.1 = (bf16[32,12,128]{2,1,0:T(8,128)(2,1)S(1)}, bf16[32,12,128]{2,1,0:T(8,128)(2,1)S(1)}, u32[]{:S(2)}, u32[]{:S(2)}) collective-permute-start(bf16[32,12,128]{2,1,0:T(8,128)(2,1)S(1)} %get-tuple-element.17), channel_id=1, source_target_pairs={{0,124},{4,8},{8,4},{12,16},{16,12},{20,24},{24,20},{28,32},{32,28... | collective-permute-start | bytes 294920 | tf_op jit(solution)/shard_map/ppermute | solution.py:329
  4.5 0.7 copy-start.6
  5.4 0.7 copy-start.7
  6.3 1.3 %copy-start.5 = (bf16[32,24,128]{2,1,0:T(8,128)(2,1)S(1)}, bf16[32,24,128]{2,1,0:T(8,128)(2,1)}, u32[]{:S(2)}) copy-start(bf16[32,24,128]{2,1,0:T(8,128)(2,1)} %param.10) | copy-start | bytes 589828
  7.6 4.2 %copy-start.2 = (bf16[768,256]{1,0:T(8,128)(2,1)S(1)}, bf16[768,256]{1,0:T(8,128)(2,1)}, u32[]{:S(2)}) copy-start(bf16[768,256]{1,0:T(8,128)(2,1)} %constant.40.clone.wz_ref) | copy-start | bytes 1179652
  7.6 4.1 %copy-start.1 = (bf16[6,256,256]{2,1,0:T(8,128)(2,1)S(1)}, bf16[6,256,256]{2,1,0:T(8,128)(2,1)}, u32[]{:S(2)}) copy-start(bf16[6,256,256]{2,1,0:T(8,128)(2,1)} %constant.42.clone.wx_ref) | copy-start | bytes 2359300
  7.8 4.0 %copy-start = (s32[32,24,128]{2,1,0:T(8,128)S(1)}, s32[32,24,128]{2,1,0:T(8,128)}, u32[]{:S(2)}) copy-start(s32[32,24,128]{2,1,0:T(8,128)} %labels_ref.3) | copy-start | bytes 1179652
  7.8 4.0 %copy-start.4 = (bf16[2,80,144]{2,1,0:T(8,128)(2,1)S(1)}, bf16[2,80,144]{2,1,0:T(8,128)(2,1)}, u32[]{:S(2)}) copy-start(bf16[2,80,144]{2,1,0:T(8,128)(2,1)} %constant.41.clone.wy_ref) | copy-start | bytes 138244
  7.8 12.2 %collective-permute-start.3 = (bf16[12,48,128]{2,1,0:T(8,128)(2,1)S(1)}, bf16[12,48,128]{2,1,0:T(8,128)(2,1)S(1)}, u32[]{:S(2)}, u32[]{:S(2)}) collective-permute-start(bf16[12,48,128]{2,1,0:T(8,128)(2,1)S(1)} %get-tuple-element.12), channel_id=1, source_target_pairs={{1,0},{2,1},{3,2},{0,3},{5,4},{6,5},{7,6},{4,7},{9,8},{10,9},{11,1... | collective-permute-start | bytes 442376 | tf_op jit(solution)/shard_map/ppermute | solution.py:318
  11.7 8.3 %copy-start.3 = (bf16[576,240]{1,0:T(8,128)(2,1)S(1)}, bf16[576,240]{1,0:T(8,128)(2,1)}, u32[]{:S(2)}) copy-start(bf16[576,240]{1,0:T(8,128)(2,1)} %constant.43.clone.wz_ref) | copy-start | bytes 829444
  11.7 8.3 %collective-permute-start.2 = (bf16[12,48,128]{2,1,0:T(8,128)(2,1)S(1)}, bf16[12,48,128]{2,1,0:T(8,128)(2,1)S(1)}, u32[]{:S(2)}, u32[]{:S(2)}) collective-permute-start(bf16[12,48,128]{2,1,0:T(8,128)(2,1)S(1)} %get-tuple-element.13), channel_id=1, source_target_pairs={{0,1},{1,2},{2,3},{3,0},{4,5},{5,6},{6,7},{7,4},{8,9},{9,10},{10,1... | collective-permute-start | bytes 442376 | tf_op jit(solution)/shard_map/ppermute | solution.py:318

commit v7 on v5

--- a/solution.py
+++ b/solution.py
@@ -20,7 +20,7 @@
 ORDERS = ((2, 0, 0), (0, 2, 0), (0, 0, 2), (1, 1, 0), (1, 0, 1), (0, 1, 1))
 HI = 8
 LO = 256
-SEND = 24
+SEND = 5
 F32, BF16 = jnp.float32, jnp.bfloat16
 
 
@@ -277,34 +277,37 @@
                     pl.ds((slot % 2) * LBL, LBL),
                 ]
         for quarter in range(4):
-            send_ref[owner, quarter, pl.ds(0, 16), :] = turned[pl.ds(16 * quarter, 16), :].astype(
-                BF16
-            )
-            send_ref[owner, quarter, pl.ds(16, 8), :] = jnp.full((8, LBL), rank, F32).astype(BF16)
+            for part in range(4):
+                send_ref[owner, quarter, part] = turned[
+                    pl.ds(16 * quarter + 4 * part, 4), :
+                ].astype(BF16)
+            send_ref[owner, quarter, 4] = jnp.full((4, LBL), rank, F32).astype(BF16)
     for index in range(count):
         like_copy(index).wait()
     inner_copy.wait()
 
 
 def sum_kernel(got_ref, out_ref):
-    sources = got_ref.shape[0]
+    sources, parts = (got_ref.shape[0], got_ref.shape[1] - 1)
 
     def step(source, totals):
-        block = got_ref[source].astype(F32)
-        data, rank = (block[:16], jnp.concatenate([block[16:], block[16:]], axis=0))
+        rank = got_ref[source, parts].astype(F32)
+        data = [got_ref[source, part].astype(F32) for part in range(parts)]
         return tuple(
-            total + jnp.where(rank == float(index), data, 0.0) for index, total in enumerate(totals)
+            tuple(
+                total + jnp.where(rank == float(index), block, 0.0)
+                for total, block in zip(row, data)
+            )
+            for index, row in enumerate(totals)
         )
 
+    zero = jnp.zeros((4, LBL), F32)
     totals = lax.fori_loop(
-        0,
-        sources,
-        step,
-        tuple(jnp.zeros(out_ref.shape[1:], F32) for _ in range(out_ref.shape[0])),
-        unroll=8,
-    )
-    for index, total in enumerate(totals):
-        out_ref[index] = total
+        0, sources, step, ((zero,) * parts,) * out_ref.shape[0], unroll=8
+    )
+    for index, row in enumerate(totals):
+        for part, total in enumerate(row):
+            out_ref[index, pl.ds(4 * part, 4)] = total
 
 
 def neighbours(shard, axis, dim, width):
@@ -366,7 +369,7 @@
         outer_kernel,
         out_shape=(
             jax.ShapeDtypeStruct(labels.shape, BF16),
-            jax.ShapeDtypeStruct((groups, quarters, SEND, LBL), BF16),
+            jax.ShapeDtypeStruct((groups, quarters, SEND, 4, LBL), BF16),
         ),
         in_specs=[SMEM] * 3 + [VMEM] * 9,
         out_specs=(pl.BlockSpec(memory_space=pl.ANY), VMEM),
@@ -409,7 +412,7 @@
         owners, ranks, jnp.stack(ends).astype(jnp.int32), before, own, after, labels, inner,
         groups, quarters,
     )
-    message = message.reshape(groups * quarters, SEND, LBL)
+    message = message.reshape(groups * quarters, SEND, 4, LBL)
     got = lax.all_to_all(message, ("gy", "gz"), 0, 0, tiled=True)
     label_features = pl.pallas_call(
         sum_kernel,

time: 74.1 us -> 73.1 us (0.987)
  blocking collectives: 26.7 us -> 25.3 us
    all_to_all x1, blocking collectives: 26.7 us -> 25.3 us  [local(): got = lax.all_to_all(message, ('gy', 'gz'), 0, 0, tiled=True)]
where the time goes in v7:
time: 73.1 us; the launch traced here: 72.9 us
  Pallas kernels  34.4 us (47%)
  blocking collectives  25.3 us (35%)
  starting transfers between devices  6.59 us (9%)
  waiting for transfers between devices  2.92 us (4%)
  local copies, waits for them, and re-layouts  2.39 us (3%)
  between operations  0.77 us (1%)
    all_to_all x1, blocking collectives, local(): got = lax.all_to_all(message, ('gy', 'gz'), 0, 0, tiled=True)  25.3 us
    pallas_call x1, Pallas kernels, outer_sums(): pl.pallas_call(outer_kernel, out_shape=(jax.ShapeDtypeStruct(labels.shape...  24.7 us
    pallas_call x1, Pallas kernels, inner_sums(): pl.pallas_call(inner_kernel, out_shape=(jax.ShapeDtypeStruct(labels.shape...  8.22 us
    ppermute x2, starting transfers between devices, neighbours(): lax.ppermute(leading, axis, down)  3.83 us
    ppermute x2, starting transfers between devices, neighbours(): lax.ppermute(last, axis, up)  2.76 us
    ppermute x2, waiting for transfers between devices, neighbours(): lax.ppermute(leading, axis, down)  2.72 us
  transfers between devices with their start and end apart: 4, of which 2 were waited for; matrix products, arithmetic and copies ran while one was open for 1% of the time, Pallas kernels for 11%

profile of v7, /device:TPU:1, one launch (start us, length us, event | category | flops | bytes accessed | tf_op | source)
XLA Modules:
  0.0 72.9 jit_solution(10280394081385624621)
XLA Ops:
  0.6 1.0 %fusion.2 = (bf16[32,12,128]{2,1,0:T(8,128)(2,1)S(1)}, bf16[32,12,128]{2,1,0:T(8,128)(2,1)S(1)}) fusion(bf16[32,24,128]{2,1,0:T(8,128)(2,1)} %param.10), kind=kLoop, calls=%fused_computation.11 | loop fusion | bytes 393216 | tf_op jit(solution)/shard_map/slice | solution.py:317
  1.7 2.8 %collective-permute-start = (bf16[32,12,128]{2,1,0:T(8,128)(2,1)S(1)}, bf16[32,12,128]{2,1,0:T(8,128)(2,1)S(1)}, u32[]{:S(2)}, u32[]{:S(2)}) collective-permute-start(bf16[32,12,128]{2,1,0:T(8,128)(2,1)S(1)} %get-tuple-element.14), channel_id=1, source_target_pairs={{0,4},{4,8},{8,12},{12,16},{16,20},{20,24},{24,28},{28,32},{32,36}... | collective-permute-start | bytes 294920 | tf_op jit(solution)/shard_map/ppermute | solution.py:321
  4.4 0.0 collective-permute-start.1
  4.4 0.0 copy-start.6
  4.4 0.7 copy-done.6
  5.1 0.2 convert_reduce_fusion
  5.2 0.0 copy-start.7
  5.3 0.7 copy-done.7
  5.9 0.2 select_reduce_fusion
  6.1 0.1 add_convert_fusion.ends_ref
  6.2 0.2 collective-permute-done
  6.4 0.0 copy-start.5
  6.4 2.7 %collective-permute-done.1 = bf16[32,12,128]{2,1,0:T(8,128)(2,1)S(1)} collective-permute-done((bf16[32,12,128]{2,1,0:T(8,128)(2,1)S(1)}, bf16[32,12,128]{2,1,0:T(8,128)(2,1)S(1)}, u32[]{:S(2)}, u32[]{:S(2)}) %collective-permute-start.1) | collective-permute-done | bytes 98336 | tf_op jit(solution)/shard_map/ppermute | solution.py:321
  9.1 0.0 copy-start.2
  9.1 0.0 copy-done.5
  9.1 0.0 copy-start.1
  9.1 0.1 pad_maximum_fusion.own_ref
  9.3 0.0 copy-start
  9.3 0.0 copy-start.4
  9.3 3.8 %collective-permute-start.3 = (bf16[12,48,128]{2,1,0:T(8,128)(2,1)S(1)}, bf16[12,48,128]{2,1,0:T(8,128)(2,1)S(1)}, u32[]{:S(2)}, u32[]{:S(2)}) collective-permute-start(bf16[12,48,128]{2,1,0:T(8,128)(2,1)S(1)} %get-tuple-element.12), channel_id=1, source_target_pairs={{1,0},{2,1},{3,2},{0,3},{5,4},{6,5},{7,6},{4,7},{9,8},{10,9},{11,1... | collective-permute-start | bytes 442376 | tf_op jit(solution)/shard_map/ppermute | solution.py:321
  13.2 0.0 copy-start.3
  13.2 0.0 collective-permute-start.2
  13.2 0.0 copy-done.2
  13.2 0.0 copy-done.1
  13.2 0.0 copy-done
  13.2 0.0 copy-done.4
  13.2 8.2 %shard_map.113 = (bf16[32,24,128]{2,1,0:T(8,128)(2,1)S(1)}, f32[512,256]{1,0:T(8,128)S(1)}) custom-call(bf16[32,48,128]{2,1,0:T(8,128)(2,1)S(1)} %pad_maximum_fusion.own_ref, s32[32,24,128]{2,1,0:T(8,128)S(1)} %copy-done, bf16[768,256]{1,0:T(8,128)(2,1)S(1)} %copy-done.2, bf16[2,80,144]{2,1,0:T(8,128)(2,1)S(1)} %copy-done.4, bf16[6,256,256]{2,1,0:T(8,128)(2,1)S(1)} %copy-done.1), custom_call_target="tpu_custom_call" | custom-call | flops 7000000000 | bytes 1000000 | tf_op jit(solution)/shard_map/pallas_call | solution.py:352
  21.4 0.0 collective-permute-done.3.after_ref
  21.4 0.0 collective-permute-done.2.before_ref
  21.5 0.0 copy-done.3
  21.5 24.7 %shard_map.114 = (bf16[32,24,128]{2,1,0:T(8,128)(2,1)}, bf16[32,4,5,4,128]{4,3,2,1,0:T(4,128)(2,1)S(1)}) custom-call(s32[16]{0:T(128)S(1)} %get-tuple-element.11.owner_ref, s32[16]{0:T(128)S(1)} %get-tuple-element.10.rank_ref, s32[2]{0:T(128)S(1)} %add_convert_fusion.ends_ref, bf16[12,48,128]{2,1,0:T(8,128)(2,1)S(1)} %collective-permute-done.2.before_ref, ...), custom_call_target="tpu_custom_call" | custom-call | flops 20999999488 | bytes 3000000 | tf_op jit(solution)/shard_map/pallas_call | solution.py:368
  46.2 25.3 %all_to_all.5.got_ref = bf16[128,5,4,128]{3,2,1,0:T(4,128)(2,1)S(1)} all-to-all(bf16[128,5,4,128]{3,2,1,0:T(4,128)(2,1)S(1)} %bitcast.4), channel_id=1, replica_groups=mesh['gy'=32,'gz'=4] {'gy','gz'}, dimensions={0} | all-to-all | bytes 1310720 | tf_op jit(solution)/shard_map/all_to_all | solution.py:416
  71.6 1.4 %shard_map.115 = f32[4,16,128]{2,1,0:T(8,128)} custom-call(bf16[128,5,4,128]{3,2,1,0:T(4,128)(2,1)S(1)} %all_to_all.5.got_ref), custom_call_target="tpu_custom_call" | custom-call | tf_op jit(solution)/shard_map/pallas_call | solution.py:417
  (3 shorter events, 0.0 us)
Async XLA Ops:
  1.7 4.7 %collective-permute-start = (bf16[32,12,128]{2,1,0:T(8,128)(2,1)S(1)}, bf16[32,12,128]{2,1,0:T(8,128)(2,1)S(1)}, u32[]{:S(2)}, u32[]{:S(2)}) collective-permute-start(bf16[32,12,128]{2,1,0:T(8,128)(2,1)S(1)} %get-tuple-element.14), channel_id=1, source_target_pairs={{0,4},{4,8},{8,12},{12,16},{16,20},{20,24},{24,28},{28,32},{32,36}... | collective-permute-start | bytes 294920 | tf_op jit(solution)/shard_map/ppermute | solution.py:321
  4.4 4.7 %collective-permute-start.1 = (bf16[32,12,128]{2,1,0:T(8,128)(2,1)S(1)}, bf16[32,12,128]{2,1,0:T(8,128)(2,1)S(1)}, u32[]{:S(2)}, u32[]{:S(2)}) collective-permute-start(bf16[32,12,128]{2,1,0:T(8,128)(2,1)S(1)} %get-tuple-element.15), channel_id=1, source_target_pairs={{4,0},{8,4},{12,8},{16,12},{20,16},{24,20},{28,24},{32,28},{36,32}... | collective-permute-start | bytes 294920 | tf_op jit(solution)/shard_map/ppermute | solution.py:321
  4.4 0.7 copy-start.6
  5.2 0.7 copy-start.7
  6.4 2.8 %copy-start.5 = (bf16[32,24,128]{2,1,0:T(8,128)(2,1)S(1)}, bf16[32,24,128]{2,1,0:T(8,128)(2,1)}, u32[]{:S(2)}) copy-start(bf16[32,24,128]{2,1,0:T(8,128)(2,1)} %param.10) | copy-start | bytes 589828
  9.1 4.1 %copy-start.2 = (bf16[768,256]{1,0:T(8,128)(2,1)S(1)}, bf16[768,256]{1,0:T(8,128)(2,1)}, u32[]{:S(2)}) copy-start(bf16[768,256]{1,0:T(8,128)(2,1)} %constant.27.clone.wz_ref) | copy-start | bytes 1179652
  9.1 4.0 %copy-start.1 = (bf16[6,256,256]{2,1,0:T(8,128)(2,1)S(1)}, bf16[6,256,256]{2,1,0:T(8,128)(2,1)}, u32[]{:S(2)}) copy-start(bf16[6,256,256]{2,1,0:T(8,128)(2,1)} %constant.29.clone.wx_ref) | copy-start | bytes 2359300
  9.3 3.9 %copy-start = (s32[32,24,128]{2,1,0:T(8,128)S(1)}, s32[32,24,128]{2,1,0:T(8,128)}, u32[]{:S(2)}) copy-start(s32[32,24,128]{2,1,0:T(8,128)} %labels_ref.3) | copy-start | bytes 1179652
  9.3 3.9 %copy-start.4 = (bf16[2,80,144]{2,1,0:T(8,128)(2,1)S(1)}, bf16[2,80,144]{2,1,0:T(8,128)(2,1)}, u32[]{:S(2)}) copy-start(bf16[2,80,144]{2,1,0:T(8,128)(2,1)} %constant.28.clone.wy_ref) | copy-start | bytes 138244
  9.3 12.1 %collective-permute-start.3 = (bf16[12,48,128]{2,1,0:T(8,128)(2,1)S(1)}, bf16[12,48,128]{2,1,0:T(8,128)(2,1)S(1)}, u32[]{:S(2)}, u32[]{:S(2)}) collective-permute-start(bf16[12,48,128]{2,1,0:T(8,128)(2,1)S(1)} %get-tuple-element.12), channel_id=1, source_target_pairs={{1,0},{2,1},{3,2},{0,3},{5,4},{6,5},{7,6},{4,7},{9,8},{10,9},{11,1... | collective-permute-start | bytes 442376 | tf_op jit(solution)/shard_map/ppermute | solution.py:321
  13.2 8.3 %copy-start.3 = (bf16[576,240]{1,0:T(8,128)(2,1)S(1)}, bf16[576,240]{1,0:T(8,128)(2,1)}, u32[]{:S(2)}) copy-start(bf16[576,240]{1,0:T(8,128)(2,1)} %constant.30.clone.wz_ref) | copy-start | bytes 829444
  13.2 8.3 %collective-permute-start.2 = (bf16[12,48,128]{2,1,0:T(8,128)(2,1)S(1)}, bf16[12,48,128]{2,1,0:T(8,128)(2,1)S(1)}, u32[]{:S(2)}, u32[]{:S(2)}) collective-permute-start(bf16[12,48,128]{2,1,0:T(8,128)(2,1)S(1)} %get-tuple-element.13), channel_id=1, source_target_pairs={{0,1},{1,2},{2,3},{3,0},{4,5},{5,6},{6,7},{7,4},{8,9},{9,10},{10,1... | collective-permute-start | bytes 442376 | tf_op jit(solution)/shard_map/ppermute | solution.py:321

commit v8 on v7

--- a/solution.py
+++ b/solution.py
@@ -121,20 +121,29 @@
                     component = [
                         i for i, o in enumerate(ORDERS) if o[1:] == (order_y, order_z)
                     ][0]
-                    for half in range(2):
+                    both = jnp.concatenate(
+                        [
+                            out[
+                                order_y * rows_y : (order_y + 1) * rows_y,
+                                half * width : (half + 1) * width,
+                            ]
+                            for half in range(2)
+                        ],
+                        axis=0,
+                    )
+                    for index, part in enumerate(split(both)):
                         y_out[
-                            scale * 6 + component, pl.ds((2 * pair + half) * rows_y, rows_y), :
-                        ] = out[
-                            order_y * rows_y : (order_y + 1) * rows_y,
-                            half * width : (half + 1) * width,
-                        ]
+                            scale * 6 + component,
+                            pl.ds(2 * pair * rows_y, 2 * rows_y),
+                            pl.ds(index * width, width),
+                        ] = part
 
     tubes = []
     for scale in range(2):
         hessian = [None] * 6
         for order_x in range(3):
             members = [i for i, o in enumerate(ORDERS) if o[0] == order_x]
-            two = [jnp.concatenate(split(y_out[scale * 6 + i]), axis=1) for i in members]
+            two = [y_out[scale * 6 + i] for i in members]
             out = jnp.dot(
                 jnp.concatenate(two, axis=0),
                 wx_ref[scale * 3 + order_x],
@@ -332,7 +341,7 @@
         pltpu.VMEM((slab_z + 2 * HALO, deep, width), F32),
         pltpu.VMEM((6, chunk, deep, width), BF16),
         pltpu.VMEM((6, chunk, deep, width), BF16),
-        pltpu.VMEM((12, rows, width), F32),
+        pltpu.VMEM((12, rows, 2 * width), BF16),
         pltpu.VMEM((16 * rows, width), F32),
         pltpu.VMEM((4 * rows, width), F32),
     ]

time: 73.1 us -> 73.1 us (level)
  no operation moved by 1% of the time
where the time goes in v8:
time: 73.1 us; the launch traced here: 72.9 us
  Pallas kernels  34.3 us (47%)
  blocking collectives  25.3 us (35%)
  starting transfers between devices  6.59 us (9%)
  waiting for transfers between devices  2.92 us (4%)
  local copies, waits for them, and re-layouts  2.39 us (3%)
  between operations  0.77 us (1%)
    all_to_all x1, blocking collectives, local(): got = lax.all_to_all(message, ('gy', 'gz'), 0, 0, tiled=True)  25.3 us
    pallas_call x1, Pallas kernels, outer_sums(): pl.pallas_call(outer_kernel, out_shape=(jax.ShapeDtypeStruct(labels.shape...  24.7 us
    pallas_call x1, Pallas kernels, inner_sums(): pl.pallas_call(inner_kernel, out_shape=(jax.ShapeDtypeStruct(labels.shape...  8.23 us
    ppermute x2, starting transfers between devices, neighbours(): lax.ppermute(leading, axis, down)  3.83 us
    ppermute x2, starting transfers between devices, neighbours(): lax.ppermute(last, axis, up)  2.76 us
    ppermute x2, waiting for transfers between devices, neighbours(): lax.ppermute(leading, axis, down)  2.72 us
  transfers between devices with their start and end apart: 4, of which 2 were waited for; matrix products, arithmetic and copies ran while one was open for 1% of the time, Pallas kernels for 11%

profile of v8, /device:TPU:1, one launch (start us, length us, event | category | flops | bytes accessed | tf_op | source)
XLA Modules:
  0.0 72.9 jit_solution(12841578852309261541)
XLA Ops:
  0.6 1.0 %fusion.2 = (bf16[32,12,128]{2,1,0:T(8,128)(2,1)S(1)}, bf16[32,12,128]{2,1,0:T(8,128)(2,1)S(1)}) fusion(bf16[32,24,128]{2,1,0:T(8,128)(2,1)} %param.10), kind=kLoop, calls=%fused_computation.11 | loop fusion | bytes 393216 | tf_op jit(solution)/shard_map/slice | solution.py:326
  1.7 2.8 %collective-permute-start = (bf16[32,12,128]{2,1,0:T(8,128)(2,1)S(1)}, bf16[32,12,128]{2,1,0:T(8,128)(2,1)S(1)}, u32[]{:S(2)}, u32[]{:S(2)}) collective-permute-start(bf16[32,12,128]{2,1,0:T(8,128)(2,1)S(1)} %get-tuple-element.14), channel_id=1, source_target_pairs={{0,4},{4,8},{8,12},{12,16},{16,20},{20,24},{24,28},{28,32},{32,36}... | collective-permute-start | bytes 294920 | tf_op jit(solution)/shard_map/ppermute | solution.py:330
  4.4 0.0 collective-permute-start.1
  4.4 0.0 copy-start.6
  4.4 0.7 copy-done.6
  5.1 0.2 convert_reduce_fusion
  5.2 0.0 copy-start.7
  5.3 0.7 copy-done.7
  5.9 0.2 select_reduce_fusion
  6.1 0.1 add_convert_fusion.ends_ref
  6.2 0.2 collective-permute-done
  6.4 0.0 copy-start.5
  6.4 2.7 %collective-permute-done.1 = bf16[32,12,128]{2,1,0:T(8,128)(2,1)S(1)} collective-permute-done((bf16[32,12,128]{2,1,0:T(8,128)(2,1)S(1)}, bf16[32,12,128]{2,1,0:T(8,128)(2,1)S(1)}, u32[]{:S(2)}, u32[]{:S(2)}) %collective-permute-start.1) | collective-permute-done | bytes 98336 | tf_op jit(solution)/shard_map/ppermute | solution.py:330
  9.1 0.0 copy-start.2
  9.1 0.0 copy-done.5
  9.1 0.0 copy-start.1
  9.1 0.1 pad_maximum_fusion.own_ref
  9.3 0.0 copy-start
  9.3 0.0 copy-start.4
  9.3 3.8 %collective-permute-start.3 = (bf16[12,48,128]{2,1,0:T(8,128)(2,1)S(1)}, bf16[12,48,128]{2,1,0:T(8,128)(2,1)S(1)}, u32[]{:S(2)}, u32[]{:S(2)}) collective-permute-start(bf16[12,48,128]{2,1,0:T(8,128)(2,1)S(1)} %get-tuple-element.12), channel_id=1, source_target_pairs={{1,0},{2,1},{3,2},{0,3},{5,4},{6,5},{7,6},{4,7},{9,8},{10,9},{11,1... | collective-permute-start | bytes 442376 | tf_op jit(solution)/shard_map/ppermute | solution.py:330
  13.2 0.0 copy-start.3
  13.2 0.0 collective-permute-start.2
  13.2 0.0 copy-done.2
  13.2 0.0 copy-done.1
  13.2 0.0 copy-done
  13.2 0.0 copy-done.4
  13.2 8.2 %shard_map.113 = (bf16[32,24,128]{2,1,0:T(8,128)(2,1)S(1)}, f32[512,256]{1,0:T(8,128)S(1)}) custom-call(bf16[32,48,128]{2,1,0:T(8,128)(2,1)S(1)} %pad_maximum_fusion.own_ref, s32[32,24,128]{2,1,0:T(8,128)S(1)} %copy-done, bf16[768,256]{1,0:T(8,128)(2,1)S(1)} %copy-done.2, bf16[2,80,144]{2,1,0:T(8,128)(2,1)S(1)} %copy-done.4, bf16[6,256,256]{2,1,0:T(8,128)(2,1)S(1)} %copy-done.1), custom_call_target="tpu_custom_call" | custom-call | flops 7000000000 | bytes 1000000 | tf_op jit(solution)/shard_map/pallas_call | solution.py:361
  21.4 0.0 collective-permute-done.3.after_ref
  21.5 0.0 collective-permute-done.2.before_ref
  21.5 0.0 copy-done.3
  21.5 24.7 %shard_map.114 = (bf16[32,24,128]{2,1,0:T(8,128)(2,1)}, bf16[32,4,5,4,128]{4,3,2,1,0:T(4,128)(2,1)S(1)}) custom-call(s32[16]{0:T(128)S(1)} %get-tuple-element.11.owner_ref, s32[16]{0:T(128)S(1)} %get-tuple-element.10.rank_ref, s32[2]{0:T(128)S(1)} %add_convert_fusion.ends_ref, bf16[12,48,128]{2,1,0:T(8,128)(2,1)S(1)} %collective-permute-done.2.before_ref, ...), custom_call_target="tpu_custom_call" | custom-call | flops 20999999488 | bytes 3000000 | tf_op jit(solution)/shard_map/pallas_call | solution.py:377
  46.2 25.3 %all_to_all.5.got_ref = bf16[128,5,4,128]{3,2,1,0:T(4,128)(2,1)S(1)} all-to-all(bf16[128,5,4,128]{3,2,1,0:T(4,128)(2,1)S(1)} %bitcast.4), channel_id=1, replica_groups=mesh['gy'=32,'gz'=4] {'gy','gz'}, dimensions={0} | all-to-all | bytes 1310720 | tf_op jit(solution)/shard_map/all_to_all | solution.py:425
  71.6 1.4 %shard_map.115 = f32[4,16,128]{2,1,0:T(8,128)} custom-call(bf16[128,5,4,128]{3,2,1,0:T(4,128)(2,1)S(1)} %all_to_all.5.got_ref), custom_call_target="tpu_custom_call" | custom-call | tf_op jit(solution)/shard_map/pallas_call | solution.py:426
  (3 shorter events, 0.0 us)
Async XLA Ops:
  1.7 4.7 %collective-permute-start = (bf16[32,12,128]{2,1,0:T(8,128)(2,1)S(1)}, bf16[32,12,128]{2,1,0:T(8,128)(2,1)S(1)}, u32[]{:S(2)}, u32[]{:S(2)}) collective-permute-start(bf16[32,12,128]{2,1,0:T(8,128)(2,1)S(1)} %get-tuple-element.14), channel_id=1, source_target_pairs={{0,4},{4,8},{8,12},{12,16},{16,20},{20,24},{24,28},{28,32},{32,36}... | collective-permute-start | bytes 294920 | tf_op jit(solution)/shard_map/ppermute | solution.py:330
  4.4 4.7 %collective-permute-start.1 = (bf16[32,12,128]{2,1,0:T(8,128)(2,1)S(1)}, bf16[32,12,128]{2,1,0:T(8,128)(2,1)S(1)}, u32[]{:S(2)}, u32[]{:S(2)}) collective-permute-start(bf16[32,12,128]{2,1,0:T(8,128)(2,1)S(1)} %get-tuple-element.15), channel_id=1, source_target_pairs={{4,0},{8,4},{12,8},{16,12},{20,16},{24,20},{28,24},{32,28},{36,32}... | collective-permute-start | bytes 294920 | tf_op jit(solution)/shard_map/ppermute | solution.py:330
  4.4 0.7 copy-start.6
  5.2 0.7 copy-start.7
  6.4 2.8 %copy-start.5 = (bf16[32,24,128]{2,1,0:T(8,128)(2,1)S(1)}, bf16[32,24,128]{2,1,0:T(8,128)(2,1)}, u32[]{:S(2)}) copy-start(bf16[32,24,128]{2,1,0:T(8,128)(2,1)} %param.10) | copy-start | bytes 589828
  9.1 4.1 %copy-start.2 = (bf16[768,256]{1,0:T(8,128)(2,1)S(1)}, bf16[768,256]{1,0:T(8,128)(2,1)}, u32[]{:S(2)}) copy-start(bf16[768,256]{1,0:T(8,128)(2,1)} %constant.27.clone.wz_ref) | copy-start | bytes 1179652
  9.1 4.0 %copy-start.1 = (bf16[6,256,256]{2,1,0:T(8,128)(2,1)S(1)}, bf16[6,256,256]{2,1,0:T(8,128)(2,1)}, u32[]{:S(2)}) copy-start(bf16[6,256,256]{2,1,0:T(8,128)(2,1)} %constant.29.clone.wx_ref) | copy-start | bytes 2359300
  9.3 3.9 %copy-start = (s32[32,24,128]{2,1,0:T(8,128)S(1)}, s32[32,24,128]{2,1,0:T(8,128)}, u32[]{:S(2)}) copy-start(s32[32,24,128]{2,1,0:T(8,128)} %labels_ref.3) | copy-start | bytes 1179652
  9.3 3.9 %copy-start.4 = (bf16[2,80,144]{2,1,0:T(8,128)(2,1)S(1)}, bf16[2,80,144]{2,1,0:T(8,128)(2,1)}, u32[]{:S(2)}) copy-start(bf16[2,80,144]{2,1,0:T(8,128)(2,1)} %constant.28.clone.wy_ref) | copy-start | bytes 138244
  9.3 12.1 %collective-permute-start.3 = (bf16[12,48,128]{2,1,0:T(8,128)(2,1)S(1)}, bf16[12,48,128]{2,1,0:T(8,128)(2,1)S(1)}, u32[]{:S(2)}, u32[]{:S(2)}) collective-permute-start(bf16[12,48,128]{2,1,0:T(8,128)(2,1)S(1)} %get-tuple-element.12), channel_id=1, source_target_pairs={{1,0},{2,1},{3,2},{0,3},{5,4},{6,5},{7,6},{4,7},{9,8},{10,9},{11,1... | collective-permute-start | bytes 442376 | tf_op jit(solution)/shard_map/ppermute | solution.py:330
  13.2 8.3 %copy-start.3 = (bf16[576,240]{1,0:T(8,128)(2,1)S(1)}, bf16[576,240]{1,0:T(8,128)(2,1)}, u32[]{:S(2)}) copy-start(bf16[576,240]{1,0:T(8,128)(2,1)} %constant.30.clone.wz_ref) | copy-start | bytes 829444
  13.2 8.3 %collective-permute-start.2 = (bf16[12,48,128]{2,1,0:T(8,128)(2,1)S(1)}, bf16[12,48,128]{2,1,0:T(8,128)(2,1)S(1)}, u32[]{:S(2)}, u32[]{:S(2)}) collective-permute-start(bf16[12,48,128]{2,1,0:T(8,128)(2,1)S(1)} %get-tuple-element.13), channel_id=1, source_target_pairs={{0,1},{1,2},{2,3},{3,0},{4,5},{5,6},{6,7},{7,4},{8,9},{9,10},{10,1... | collective-permute-start | bytes 442376 | tf_op jit(solution)/shard_map/ppermute | solution.py:330
